TPU v7x, 32 devices: a whole 2x2x4 slice. The times are simulated.
32 devices in a mesh: tm: 8 (over z, x), frac: 4 (over y, core).
Axes of the slice: x: 2, y: 2, z: 4, core: 2. Of those that a mesh axis runs over, the one named last changes fastest.
Arguments:
- pressure0: float32 [16, 32, 128], P('frac'), may hold values from -6 to 6
- storage: float32 [16, 32, 128], P('frac'), may hold values from 0.1 to 1
- perm_base: float32 [16, 32, 128], P('frac'), may hold values from 0.2 to 5
- leakoff: float32 [16, 32, 128], P('frac'), may hold values from 0.5 to 2
- sources: float32 [8, 16, 32, 128], P('tm', 'frac'), may hold values from -6 to 6
- export_cells: int32 [1024], P('frac'), may hold values from 0 to 16383
- inter_local: int32 [4096], P('frac'), may hold values from 0 to 16383
- trace_source: int32 [4096], P('frac'), may hold values from 0 to 1023, as said below
- inter_trans: float32 [4096], P('frac'), may hold values from 0.5 to 4
- inter_count: int32 [4], P('frac'), may hold values from 1 to 1024, 2048 in all
Outputs:
- slice_pressure: float32 [8, 16, 32, 128], P('tm', 'frac')
Inputs may be any that keep to these rules, and one draw needn't show every extreme that they name: An entry of frac index d names a slot of another frac index: trace_source // 256 differs from d. `inter_count`: the live entries of a frac index are its first ones; the largest count is 1024.
All inputs are finite; a program needn't handle non-finite values. No bound on the sum of `inter_count` on one device may be relied on, other than what follows from the above.
Results may differ from a plain program's by a relative error of at most 0.00002.
Values sent between devices are 32-bit elements; how exact they have to be, the bound alone decides.
No kernel may reach another device: no remote copies, remote signals or barrier semaphores. Data moves between devices by JAX's collectives and lax.ppermute only.
A program may use at most 64 MiB of HBM per device.

v0:
```python
import jax
import jax.numpy as jnp
from jax import lax
from jax.sharding import PartitionSpec as P

FINE_STEPS = 4
SWEEPS = 8
COARSE_SWEEPS = 2
ITERS = 2


stress_factor = 0.15
fine_size = 0.25


def next_rows(array):
    return jnp.concatenate([array[:, 1:, :], jnp.zeros_like(array[:, :1, :])], axis=1)


def prev_rows(array):
    return jnp.concatenate([jnp.zeros_like(array[:, :1, :]), array[:, :-1, :]], axis=1)


def next_cols(array):
    return jnp.concatenate([array[:, :, 1:], jnp.zeros_like(array[:, :, :1])], axis=2)


def prev_cols(array):
    return jnp.concatenate([jnp.zeros_like(array[:, :, :1]), array[:, :, :-1]], axis=2)


def implicit(pressure, slice_source, step_size, sweeps, fields, couple):
    storage, perm_base, leakoff, tisum = fields
    permeability = perm_base * jnp.exp(stress_factor * pressure)
    row_index = lax.broadcasted_iota(jnp.int32, pressure.shape, 1)
    col_index = lax.broadcasted_iota(jnp.int32, pressure.shape, 2)
    face_rows = jnp.where(
        row_index < pressure.shape[1] - 1, 0.5 * (permeability + next_rows(permeability)), 0.0
    )
    face_cols = jnp.where(
        col_index < pressure.shape[2] - 1, 0.5 * (permeability + next_cols(permeability)), 0.0
    )
    storage_rate = storage / step_size
    diagonal_total = (
        storage_rate + leakoff + face_rows + prev_rows(face_rows) + face_cols + prev_cols(face_cols)
    )
    right_side = storage_rate * pressure + slice_source
    if couple is not None:
        diagonal_total = diagonal_total + tisum
        right_side = right_side + couple(pressure)

    def sweep(sweep_index, current):
        beside = face_rows * next_rows(current) + prev_rows(face_rows * current)
        beside = beside + face_cols * next_cols(current) + prev_cols(face_cols * current)
        return (right_side + beside) / diagonal_total

    return lax.fori_loop(0, sweeps, sweep, pressure)


def body(
    pressure0,
    storage,
    perm_base,
    leakoff,
    sources,
    export_cells,
    inter_local,
    trace_source,
    inter_trans,
    inter_count,
):
    slice_count = lax.axis_size("tm")
    slice_index = lax.axis_index("tm")
    own_source = sources[0]
    entry_index = lax.broadcasted_iota(jnp.int32, inter_local.shape, 0)
    weights = jnp.where(entry_index < inter_count[0], inter_trans, jnp.zeros_like(inter_trans))
    cell_total = pressure0.size
    tisum = (
        jnp.zeros((cell_total,), jnp.float32).at[inter_local].add(weights).reshape(pressure0.shape)
    )
    fields = (storage, perm_base, leakoff, tisum)

    def couple(current):
        flat_field = current.reshape(-1)
        exported = flat_field[export_cells]
        gathered = lax.all_gather(exported, "frac", axis=0, tiled=True)
        remote_values = gathered[trace_source]
        return (
            jnp.zeros_like(flat_field)
            .at[inter_local]
            .add(weights * remote_values)
            .reshape(current.shape)
        )

    def coarse(pressure, slice_source):
        return implicit(pressure, slice_source, fine_size * FINE_STEPS, COARSE_SWEEPS, fields, None)

    all_sources = lax.all_gather(sources, "tm", axis=0, tiled=True)

    def chain(correction, carry_zero):
        if carry_zero:
            all_corrections = jnp.zeros_like(all_sources)
        else:
            all_corrections = lax.all_gather(correction[None], "tm", axis=0, tiled=True)

        def turn(turn_index, carried):
            current, kept_state = carried
            slice_source = lax.dynamic_index_in_dim(all_sources, turn_index, 0, keepdims=False)
            added = lax.dynamic_index_in_dim(all_corrections, turn_index, 0, keepdims=False)
            current = coarse(current, slice_source) + added
            kept_state = jnp.where(slice_index == turn_index + 1, current, kept_state)
            return (current, kept_state)

        final_pair = lax.fori_loop(0, slice_count - 1, turn, (pressure0, pressure0))
        return final_pair[1]

    state = chain(jnp.zeros_like(pressure0), True)
    for iteration in range(ITERS):
        fine_pressure = state
        for step_number in range(FINE_STEPS):
            fine_pressure = implicit(fine_pressure, own_source, fine_size, SWEEPS, fields, couple)
        coarse_end = coarse(state, own_source)
        state = chain(fine_pressure - coarse_end, False)
    return state[None]


def solution(mesh):
    placed = (
        P("frac", None, None),
        P("frac", None, None),
        P("frac", None, None),
        P("frac", None, None),
        P("tm", "frac", None, None),
        P("frac"),
        P("frac"),
        P("frac"),
        P("frac"),
        P("frac"),
    )
    return jax.shard_map(
        body, mesh=mesh, in_specs=placed, out_specs=P("tm", "frac", None, None), check_vma=False
    )
```

profile of v0, /device:TPU:0, one launch (start us, length us, event | category | flops | bytes accessed | tf_op | source)
XLA Modules:
  0.0 279.3 jit_solution(6530419765778000673)
XLA Ops:
  0.0 0.8 copy.121
  0.9 0.8 copy-done
  1.7 0.8 copy-done.2
  2.6 33.1 %all_gather.33 = f32[8,4,32,128]{3,2,1,0:T(8,128)S(1)} all-gather(f32[1,4,32,128]{3,2,1,0:T(8,128)S(1)} %copy-done.2), channel_id=1, replica_groups=mesh['tm'=8,'frac'=4] {'tm'}, dimensions={0}, use_global_device_ids=true | all-gather | bytes 589824 | tf_op jit(solution)/shard_map/all_gather | solution.py:98
  35.7 5.6 %while.235 = (s32[]{:T(128)}, f32[4,32,128]{2,1,0:T(8,128)S(1)}, f32[4,32,128]{2,1,0:T(8,128)S(1)}, f32[4,32,128]{2,1,0:T(8,128)S(1)}, f32[4,32,128]{2,1,0:T(8,1...) while((s32[]{:T(128)}, f32[4,32,128]{2,1,0:T(8,128)S(1)}, ...), condition=%wide.region_3.4_spmd, body=%wide.region_0.3_spmd.sunk | while | flops 392741 | bytes 2790472 | solution.py:114
  36.8 0.4 while.250
  37.6 0.4 while.250
  39.2 0.4 while.250
  40.8 0.4 while.250
  41.5 0.7 copy-done.8
  42.2 1.7 gather_fusion
  44.0 5.1 %all-gather.10 = f32[4,1,256]{2,1,0:T(1,128)S(1)} all-gather(f32[1,1,256]{2,1,0:T(1,128)S(1)} %bitcast.174), channel_id=2, replica_groups=mesh['tm'=8,'frac'=4] {'frac'}, dimensions={0}, use_global_device_ids=true | all-gather | bytes 5120 | tf_op jit(solution)/shard_map/all_gather | solution.py:86
  49.1 4.5 %gather_fusion.1 = f32[1024]{0:T(1024)S(1)} fusion(f32[1024]{0:T(1024)S(1)} %bitcast.117, s32[1024]{0:T(1024)S(1)} %fusion.26), kind=kCustom, calls=%fused_computation.1 | custom fusion | bytes 12288 | tf_op jit(solution)/shard_map/gather | solution.py:87
  54.3 5.9 %scatter_custom_fusion.1 = f32[16384]{0:T(1024)S(1)} fusion(s32[1024]{0:T(1024)S(1)} %compare_select_fusion.1, f32[1024]{0:T(1024)S(1)} %get-tuple-element.1268, f32[]{:T(128)} %constant.358.clone.1), kind=kCustom, calls=%fused_computation.157 | custom fusion | flops 1024 | bytes 65540 | tf_op jit(solution)/shard_map/scatter-add | solution.py:79
  60.2 5.9 %scatter_custom_fusion = f32[16384]{0:T(1024)S(1)} fusion(s32[1024]{0:T(1024)S(1)} %compare_select_fusion.1, f32[1024]{0:T(1024)S(1)} %get-tuple-element.1267, f32[]{:T(128)} %constant.358.clone.1), kind=kCustom, calls=%fused_computation.159 | custom fusion | flops 1024 | bytes 65540 | tf_op jit(solution)/shard_map/scatter-add | solution.py:91
  66.7 1.7 while.236
  68.5 1.7 gather_fusion.2
  70.2 5.1 %all-gather.11 = f32[4,1,256]{2,1,0:T(1,128)S(1)} all-gather(f32[1,1,256]{2,1,0:T(1,128)S(1)} %bitcast.175), channel_id=3, replica_groups=mesh['tm'=8,'frac'=4] {'frac'}, dimensions={0}, use_global_device_ids=true | all-gather | bytes 5120 | tf_op jit(solution)/shard_map/all_gather | solution.py:86
  75.3 4.5 %gather_fusion.3 = f32[1024]{0:T(1024)S(1)} fusion(f32[1024]{0:T(1024)S(1)} %bitcast.119, s32[1024]{0:T(1024)S(1)} %fusion.26), kind=kCustom, calls=%fused_computation.3 | custom fusion | bytes 12288 | tf_op jit(solution)/shard_map/gather | solution.py:87
  79.8 5.9 %scatter_custom_fusion.2 = f32[16384]{0:T(1024)S(1)} fusion(s32[1024]{0:T(1024)S(1)} %compare_select_fusion.1, f32[1024]{0:T(1024)S(1)} %mul.460, f32[]{:T(128)} %constant.358.clone.1), kind=kCustom, calls=%fused_computation.155 | custom fusion | flops 1024 | bytes 65540 | tf_op jit(solution)/shard_map/scatter-add | solution.py:91
  86.1 1.7 while.237
  87.8 1.7 gather_fusion.4
  89.5 5.1 %all-gather.12 = f32[4,1,256]{2,1,0:T(1,128)S(1)} all-gather(f32[1,1,256]{2,1,0:T(1,128)S(1)} %bitcast.176), channel_id=4, replica_groups=mesh['tm'=8,'frac'=4] {'frac'}, dimensions={0}, use_global_device_ids=true | all-gather | bytes 5120 | tf_op jit(solution)/shard_map/all_gather | solution.py:86
  94.6 4.5 %gather_fusion.5 = f32[1024]{0:T(1024)S(1)} fusion(f32[1024]{0:T(1024)S(1)} %bitcast.120, s32[1024]{0:T(1024)S(1)} %fusion.26), kind=kCustom, calls=%fused_computation.5 | custom fusion | bytes 12288 | tf_op jit(solution)/shard_map/gather | solution.py:87
  99.1 5.9 %scatter_custom_fusion.3 = f32[16384]{0:T(1024)S(1)} fusion(s32[1024]{0:T(1024)S(1)} %compare_select_fusion.1, f32[1024]{0:T(1024)S(1)} %mul.466, f32[]{:T(128)} %constant.358.clone.1), kind=kCustom, calls=%fused_computation.153 | custom fusion | flops 1024 | bytes 65540 | tf_op jit(solution)/shard_map/scatter-add | solution.py:91
  105.4 1.7 while.238
  107.1 1.7 gather_fusion.6
  108.8 5.1 %all-gather.13 = f32[4,1,256]{2,1,0:T(1,128)S(1)} all-gather(f32[1,1,256]{2,1,0:T(1,128)S(1)} %bitcast.177), channel_id=5, replica_groups=mesh['tm'=8,'frac'=4] {'frac'}, dimensions={0}, use_global_device_ids=true | all-gather | bytes 5120 | tf_op jit(solution)/shard_map/all_gather | solution.py:86
  113.9 4.5 %gather_fusion.7 = f32[1024]{0:T(1024)S(1)} fusion(f32[1024]{0:T(1024)S(1)} %bitcast.121, s32[1024]{0:T(1024)S(1)} %fusion.26), kind=kCustom, calls=%fused_computation.7 | custom fusion | bytes 12288 | tf_op jit(solution)/shard_map/gather | solution.py:87
  118.4 5.9 %scatter_custom_fusion.4 = f32[16384]{0:T(1024)S(1)} fusion(s32[1024]{0:T(1024)S(1)} %compare_select_fusion.1, f32[1024]{0:T(1024)S(1)} %mul.472, f32[]{:T(128)} %constant.358.clone.1), kind=kCustom, calls=%fused_computation.151 | custom fusion | flops 1024 | bytes 65540 | tf_op jit(solution)/shard_map/scatter-add | solution.py:91
  124.7 1.7 while.239
  126.4 31.3 %all-gather.4 = f32[32,32,128]{2,1,0:T(8,128)S(1)} all-gather(f32[4,32,128]{2,1,0:T(8,128)S(1)} %sub.6), channel_id=6, replica_groups=mesh['tm'=8,'frac'=4] {'tm'}, dimensions={0}, use_global_device_ids=true | all-gather | bytes 589824 | tf_op jit(solution)/shard_map/all_gather | solution.py:104
  157.7 5.7 %while.242 = (s32[]{:T(128)}, f32[4,32,128]{2,1,0:T(8,128)S(1)}, f32[4,32,128]{2,1,0:T(8,128)S(1)}, f32[4,32,128]{2,1,0:T(8,128)S(1)}, f32[4,32,128]{2,1,0:T(8,1...) while((s32[]{:T(128)}, f32[4,32,128]{2,1,0:T(8,128)S(1)}, ...), condition=%wide.region_22.23_spmd, body=%wide.region_19.22_spmd.sunk | while | flops 409125 | bytes 2921564 | solution.py:114
  158.1 0.4 while.251
  163.4 1.7 gather_fusion.8
  165.2 5.3 %all-gather.14 = f32[4,1,256]{2,1,0:T(1,128)S(1)} all-gather(f32[1,1,256]{2,1,0:T(1,128)S(1)} %bitcast.178), channel_id=7, replica_groups=mesh['tm'=8,'frac'=4] {'frac'}, dimensions={0}, use_global_device_ids=true | all-gather | bytes 5120 | tf_op jit(solution)/shard_map/all_gather | solution.py:86
  170.4 4.5 %gather_fusion.9 = f32[1024]{0:T(1024)S(1)} fusion(f32[1024]{0:T(1024)S(1)} %bitcast.122, s32[1024]{0:T(1024)S(1)} %fusion.26), kind=kCustom, calls=%fused_computation.9 | custom fusion | bytes 12288 | tf_op jit(solution)/shard_map/gather | solution.py:87
  175.0 5.9 %scatter_custom_fusion.5 = f32[16384]{0:T(1024)S(1)} fusion(s32[1024]{0:T(1024)S(1)} %compare_select_fusion.1, f32[1024]{0:T(1024)S(1)} %mul.479, f32[]{:T(128)} %constant.358.clone.1), kind=kCustom, calls=%fused_computation.149 | custom fusion | flops 1024 | bytes 65540 | tf_op jit(solution)/shard_map/scatter-add | solution.py:91
  181.7 1.7 while.243
  183.4 1.7 gather_fusion.10
  185.1 5.1 %all-gather.15 = f32[4,1,256]{2,1,0:T(1,128)S(1)} all-gather(f32[1,1,256]{2,1,0:T(1,128)S(1)} %bitcast.179), channel_id=8, replica_groups=mesh['tm'=8,'frac'=4] {'frac'}, dimensions={0}, use_global_device_ids=true | all-gather | bytes 5120 | tf_op jit(solution)/shard_map/all_gather | solution.py:86
  190.2 4.5 %gather_fusion.11 = f32[1024]{0:T(1024)S(1)} fusion(f32[1024]{0:T(1024)S(1)} %bitcast.123, s32[1024]{0:T(1024)S(1)} %fusion.26), kind=kCustom, calls=%fused_computation.11 | custom fusion | bytes 12288 | tf_op jit(solution)/shard_map/gather | solution.py:87
  194.7 5.9 %scatter_custom_fusion.6 = f32[16384]{0:T(1024)S(1)} fusion(s32[1024]{0:T(1024)S(1)} %compare_select_fusion.1, f32[1024]{0:T(1024)S(1)} %mul.485, f32[]{:T(128)} %constant.358.clone.1), kind=kCustom, calls=%fused_computation.147 | custom fusion | flops 1024 | bytes 65540 | tf_op jit(solution)/shard_map/scatter-add | solution.py:91
  201.0 1.7 while.244
  202.7 1.7 gather_fusion.12
  204.4 5.1 %all-gather.16 = f32[4,1,256]{2,1,0:T(1,128)S(1)} all-gather(f32[1,1,256]{2,1,0:T(1,128)S(1)} %bitcast.180), channel_id=9, replica_groups=mesh['tm'=8,'frac'=4] {'frac'}, dimensions={0}, use_global_device_ids=true | all-gather | bytes 5120 | tf_op jit(solution)/shard_map/all_gather | solution.py:86
  209.5 4.5 %gather_fusion.13 = f32[1024]{0:T(1024)S(1)} fusion(f32[1024]{0:T(1024)S(1)} %bitcast.124, s32[1024]{0:T(1024)S(1)} %fusion.26), kind=kCustom, calls=%fused_computation.13 | custom fusion | bytes 12288 | tf_op jit(solution)/shard_map/gather | solution.py:87
  214.0 5.9 %scatter_custom_fusion.7 = f32[16384]{0:T(1024)S(1)} fusion(s32[1024]{0:T(1024)S(1)} %compare_select_fusion.1, f32[1024]{0:T(1024)S(1)} %mul.491, f32[]{:T(128)} %constant.358.clone.1), kind=kCustom, calls=%fused_computation.145 | custom fusion | flops 1024 | bytes 65540 | tf_op jit(solution)/shard_map/scatter-add | solution.py:91
  220.3 1.7 while.245
  222.0 1.7 gather_fusion.14
  223.7 5.1 %all-gather.17 = f32[4,1,256]{2,1,0:T(1,128)S(1)} all-gather(f32[1,1,256]{2,1,0:T(1,128)S(1)} %bitcast.173), channel_id=10, replica_groups=mesh['tm'=8,'frac'=4] {'frac'}, dimensions={0}, use_global_device_ids=true | all-gather | bytes 5120 | tf_op jit(solution)/shard_map/all_gather | solution.py:86
  228.8 4.5 %gather_fusion.15 = f32[1024]{0:T(1024)S(1)} fusion(f32[1024]{0:T(1024)S(1)} %bitcast.118, s32[1024]{0:T(1024)S(1)} %fusion.26), kind=kCustom, calls=%fused_computation.15 | custom fusion | bytes 12288 | tf_op jit(solution)/shard_map/gather | solution.py:87
  233.4 5.9 %scatter_custom_fusion.8 = f32[16384]{0:T(1024)S(1)} fusion(s32[1024]{0:T(1024)S(1)} %compare_select_fusion.1, f32[1024]{0:T(1024)S(1)} %mul.497, f32[]{:T(128)} %constant.358.clone.1), kind=kCustom, calls=%fused_computation.143 | custom fusion | flops 1024 | bytes 65540 | tf_op jit(solution)/shard_map/scatter-add | solution.py:91
  239.6 1.7 while.246
  241.4 31.6 %all-gather.9 = f32[32,32,128]{2,1,0:T(8,128)S(1)} all-gather(f32[4,32,128]{2,1,0:T(8,128)S(1)} %sub.7), channel_id=11, replica_groups=mesh['tm'=8,'frac'=4] {'tm'}, dimensions={0}, use_global_device_ids=true | all-gather | bytes 589824 | tf_op jit(solution)/shard_map/all_gather | solution.py:104
  272.9 5.7 %while.249 = (s32[]{:T(128)}, f32[4,32,128]{2,1,0:T(8,128)S(1)}, f32[4,32,128]{2,1,0:T(8,128)S(1)}, f32[4,32,128]{2,1,0:T(8,128)S(1)}, f32[4,32,128]{2,1,0:T(8,1...) while((s32[]{:T(128)}, f32[4,32,128]{2,1,0:T(8,128)S(1)}, ...), condition=%wide.region_40.41_spmd, body=%wide.region_37.40_spmd.sunk | while | flops 409125 | bytes 2921564 | solution.py:114
  273.3 0.4 while.252
  274.1 0.4 while.252
  274.9 0.4 while.252
  275.7 0.4 while.252
  276.5 0.4 while.252
  277.4 0.4 while.252
  278.2 0.4 while.252
  278.7 0.6 copy-done.3
  (587 shorter events, 34.7 us)
Async XLA Ops:
  0.8 0.8 copy-start
  0.8 0.9 copy-start.4
  1.7 0.8 copy-start.2
  2.6 33.1 %copy-start.1 = (f32[4,32,128]{2,1,0:T(8,128)S(1)}, f32[4,32,128]{2,1,0:T(8,128)}, u32[]{:S(2)}) copy-start(f32[4,32,128]{2,1,0:T(8,128)} %param.44) | copy-start | bytes 196612
  41.5 0.7 copy-start.8
  44.0 5.1 %copy-start.5 = (s32[1024]{0:T(1024)S(1)}, s32[1024]{0:T(1024)}, u32[]{:S(2)}) copy-start(s32[1024]{0:T(1024)} %param.49) | copy-start | bytes 12292
  49.0 5.2 %copy-start.7 = (f32[1024]{0:T(1024)S(1)}, f32[1024]{0:T(1024)}, u32[]{:S(2)}) copy-start(f32[1024]{0:T(1024)} %param.50) | copy-start | bytes 12292
  49.0 5.2 %copy-start.6 = (s32[1024]{0:T(1024)S(1)}, s32[1024]{0:T(1024)}, u32[]{:S(2)}) copy-start(s32[1024]{0:T(1024)} %param.48) | copy-start | bytes 12292
  278.7 0.6 copy-start.3
where the time goes:
time: 280 us; the launch traced here: 279 us
  blocking collectives  137 us (49%)
  other arithmetic  80.9 us (29%)
  local copies, waits for them, and re-layouts  56.4 us (20%)
  loops' own time  3.94 us (1%)
    all_gather x2, blocking collectives, chain(): all_corrections = lax.all_gather(correction[None], 'tm', axis=0, tiled=True)  62.9 us
    scatter-add x8, other arithmetic, couple(): return jnp.zeros_like(flat_field).at[inter_local].add(weights * remote_va...  47.6 us
    all_gather x8, blocking collectives, couple(): gathered = lax.all_gather(exported, 'frac', axis=0, tiled=True)  40.8 us
    gather x8, local copies, waits for them, and re-layouts, couple(): remote_values = gathered[trace_source]  36.2 us
    all_gather x1, blocking collectives, body(): all_sources = lax.all_gather(sources, 'tm', axis=0, tiled=True)  33.1 us
    gather x8, local copies, waits for them, and re-layouts, couple(): exported = flat_field[export_cells]  13.8 us
    div x110, other arithmetic, sweep(): return (right_side + beside) / diagonal_total  10.3 us
    slice x110, other arithmetic, next_cols(): array[:, :, 1:]  8.95 us

commit v1 on v0

v1 whole, which is shorter than its diff:
```python
import functools
import math

import jax
import jax.numpy as jnp
from jax import lax
from jax.experimental import pallas as pl
from jax.experimental.pallas import tpu as pltpu
from jax.sharding import Mesh, PartitionSpec as P

FINE_STEPS = 4
SWEEPS = 8
COARSE_SWEEPS = 2
ITERS = 2

stress_factor = 0.15
fine_size = 0.25

LANES = 128
SUBS = 8
CHUNK = 256
F32 = jnp.float32
BF16 = jnp.bfloat16
VMEM = pl.BlockSpec(memory_space=pltpu.VMEM)
HBM = pl.BlockSpec(memory_space=pltpu.HBM)
SMEM = pl.BlockSpec(memory_space=pltpu.SMEM)


def shape_of(*dims, dtype=F32):
    return jax.ShapeDtypeStruct(dims, dtype)


def call(kernel, name, args, outs, scratch=(), specs=None):
    size = sum(math.prod(a.shape) * a.dtype.itemsize for a in (*args, *outs))
    return pl.pallas_call(
        kernel,
        out_shape=outs,
        in_specs=specs or [VMEM] * len(args),
        out_specs=(VMEM,) * len(outs),
        scratch_shapes=scratch,
        compiler_params=pltpu.CompilerParams(vmem_limit_bytes=12 * 2**20 + 2 * size),
        name=name,
    )(*args)


def lane_roll(x, s):
    return pltpu.roll(x, s % LANES, axis=2)


def sub_roll(x, s):
    return pltpu.roll(x, s % SUBS, axis=1)


def implicit(q, s, c, sto, per, lea, tis, step_size, sweeps):
    J = len(q)
    shape = q[0].shape
    row = lax.broadcasted_iota(jnp.int32, shape, 1)
    col = lax.broadcasted_iota(jnp.int32, shape, 2)
    first_row, last_row, first_col, last_col = row == 0, row == SUBS - 1, col == 0, col == LANES - 1
    k = [(0.5 * per[j]) * jnp.exp(stress_factor * q[j]) for j in range(J)]
    row_next = [k[j] + k[j + 1] for j in range(J - 1)]
    edge = jnp.where(last_row, 0.0, k[J - 1] + sub_roll(k[0], -1))
    row_prev = [jnp.where(first_row, 0.0, k[0] + sub_roll(k[J - 1], 1))] + row_next
    row_next = row_next + [edge]
    col_next = [jnp.where(last_col, 0.0, k[j] + lane_roll(k[j], -1)) for j in range(J)]
    col_prev = [jnp.where(first_col, 0.0, k[j] + lane_roll(k[j], 1)) for j in range(J)]
    rhs, a_rn, a_rp, a_cn, a_cp = [], [], [], [], []
    for j in range(J):
        rate = sto[j] * (1.0 / step_size)
        total = rate + lea[j]
        b = rate * q[j] + s[j]
        if tis is not None:
            total = total + tis[j]
            b = b + c[j]
        inv = 1.0 / ((total + (row_next[j] + row_prev[j])) + (col_next[j] + col_prev[j]))
        rhs.append(b * inv)
        a_rn.append(row_next[j] * inv)
        a_rp.append(row_prev[j] * inv)
        a_cn.append(col_next[j] * inv)
        a_cp.append(col_prev[j] * inv)
    v = q
    for _ in range(sweeps):
        down = v[1:] + [sub_roll(v[0], -1)]
        up = [sub_roll(v[J - 1], 1)] + v[:-1]
        v = [
            (rhs[j] + a_rn[j] * down[j])
            + (a_rp[j] * up[j] + (a_cn[j] * lane_roll(v[j], -1) + a_cp[j] * lane_roll(v[j], 1)))
            for j in range(J)
        ]
    return v


def rows_of(ref, index, J):
    return [ref[(*index, pl.ds(j, SUBS, stride=J), slice(None))] for j in range(J)]


def put_rows(ref, index, J, parts):
    for j in range(J):
        ref[(*index, pl.ds(j, SUBS, stride=J), slice(None))] = parts[j]


def split_high_low(x, pieces):
    out = []
    for _ in range(pieces):
        part = x.astype(BF16).astype(F32)
        out.append(part)
        x = x - part
    return out


def scatter_rows(values, rt_ref, l_ref, d):
    rows = rt_ref.shape[1]
    entries = rt_ref.shape[2]
    total = jnp.zeros((len(values) * rows, LANES), F32)
    for g in range(entries // CHUNK):
        pieces = []
        for value in values:
            cols = []
            for m in range(g * CHUNK // LANES, (g + 1) * CHUNK // LANES):
                row = jnp.broadcast_to(value[m : m + 1, :], (rows, LANES)).astype(BF16)
                cols.append(rt_ref[d, :, m * LANES : (m + 1) * LANES] * row)
            pieces.append(jnp.concatenate(cols, axis=1))
        a = jnp.concatenate(pieces, axis=0)
        total = total + jnp.dot(
            a, l_ref[d, g * CHUNK : (g + 1) * CHUNK, :], preferred_element_type=F32
        )
    out = total[:rows]
    for i in range(1, len(values)):
        out = out + total[i * rows : (i + 1) * rows]
    return out


class Layout:
    def __init__(self, held, frac_rows, entries, exports):
        self.held, self.frac_rows = held, frac_rows
        self.entry_rows = entries // LANES
        self.export_rows = exports // LANES
        padded = -(-self.export_rows // SUBS) * SUBS
        self.starts = [k * self.entry_rows for k in range(4)]
        self.sizes = [self.entry_rows] * 3 + [self.export_rows]
        self.slots = 3 * held + -(-(3 * self.entry_rows + padded) // frac_rows)

    def places(self, kind):
        at, left = self.starts[kind], self.sizes[kind]
        while left:
            n = min(left, SUBS)
            yield 3 * self.held + at // self.frac_rows, at % self.frac_rows, n
            at, left = at + n, left - n

    def entries(self, ref, d, kind):
        parts = [ref[d, slot, r : r + n, :] for slot, r, n in self.places(kind)]
        return parts[0] if len(parts) == 1 else jnp.concatenate(parts, axis=0)

    def put(self, ref, kind, value):
        at = 0
        for slot, r, n in self.places(kind):
            ref[slot, r : r + n, :] = value[at : at + n]
            at += n


def pack_kernel(layout, count_ref, sto, per, lea, loc, trace, w, exp, blocks_ref, out_ref, loc_v, trace_v, w_v, exp_v, sems):
    held = layout.held
    copies = [(a, out_ref.at[pl.ds(k * held, held)]) for k, a in enumerate((sto, per, lea))]
    copies += [(loc, loc_v), (trace, trace_v), (w, w_v), (exp, exp_v)]
    copies = [pltpu.make_async_copy(a, b, sems.at[k]) for k, (a, b) in enumerate(copies)]
    for c in copies:
        c.start()
    out_ref[3 * held :] = jnp.zeros((layout.slots - 3 * held, *out_ref.shape[1:]), F32)
    for c in copies:
        c.wait()
    shape = w_v.shape
    index = lax.broadcasted_iota(jnp.int32, shape, 0) * LANES + lax.broadcasted_iota(jnp.int32, shape, 1)
    layout.put(out_ref, 0, loc_v[...].astype(F32))
    layout.put(out_ref, 1, trace_v[...].astype(F32))
    layout.put(out_ref, 2, jnp.where(index < count_ref[0], w_v[...], 0.0))
    layout.put(out_ref, 3, exp_v[...].astype(F32))


def prep_kernel(layout, *refs):
    *piece_refs, st_ref, rt_ref, l_ref, tis_ref = refs
    parts, rows, entries = rt_ref.shape
    me = lax.axis_index("frac")
    for k in range(parts):
        st_ref[lax.rem(me - k + parts, parts)] = piece_refs[k][...]
    for d in range(parts):
        cell = layout.entries(st_ref, d, 0).astype(jnp.int32)
        row, col = cell // LANES, cell % LANES
        for m in range(entries // LANES):
            at = slice(m * LANES, (m + 1) * LANES)
            iota_r = lax.broadcasted_iota(jnp.int32, (rows, LANES), 0)
            iota_l = lax.broadcasted_iota(jnp.int32, (LANES, LANES), 0)
            rt_ref[d, :, at] = jnp.where(iota_r == row[m : m + 1, :], 1.0, 0.0).astype(BF16)
            lt = jnp.where(iota_l == col[m : m + 1, :], 1.0, 0.0)
            l_ref[d, at, :] = lt.T.astype(BF16)
        tis = scatter_rows(split_high_low(layout.entries(st_ref, d, 2), 3), rt_ref, l_ref, d)
        per_part = tis_ref.shape[0] // parts
        tis_ref[d * per_part : (d + 1) * per_part] = tis.reshape(per_part, *tis_ref.shape[1:])


def couple(o_ref, c_ref, st_ref, layout, rt_ref, l_ref):
    parts, rows, _ = rt_ref.shape
    frac_rows = o_ref.shape[1]
    per_part = rows // frac_rows
    export_rows = layout.export_rows
    iota = lax.broadcasted_iota(jnp.int32, (SUBS, LANES), 0)
    exported = []
    for d in range(parts):
        cell = layout.entries(st_ref, d, 3).astype(jnp.int32)
        for e in range(export_rows):
            at = jnp.broadcast_to(cell[e : e + 1, :], (SUBS, LANES))
            row, col = at // LANES - iota, at % LANES
            found = [jnp.zeros((SUBS, LANES), F32) for _ in range(2)]
            for t in range(rows // SUBS):
                f, r = d * per_part + t * SUBS // frac_rows, t * SUBS % frac_rows
                got = jnp.take_along_axis(
                    o_ref[f, r : r + SUBS, :], col, axis=1, mode="promise_in_bounds"
                )
                found[t % 2] = jnp.where(row == t * SUBS, got, found[t % 2])
            exported.append(jnp.sum(found[0] + found[1], axis=0, keepdims=True))
    for d in range(parts):
        slot = layout.entries(st_ref, d, 1).astype(jnp.int32)
        row, col = slot // LANES, slot % LANES
        x = jnp.zeros(slot.shape, F32)
        for t in range(parts * export_rows):
            got = jnp.take_along_axis(
                jnp.broadcast_to(exported[t], slot.shape), col, axis=1, mode="promise_in_bounds"
            )
            x = jnp.where(row == t, got, x)
        c = scatter_rows(split_high_low(layout.entries(st_ref, d, 2) * x, 2), rt_ref, l_ref, d)
        c_ref[d * per_part : (d + 1) * per_part] = c.reshape(per_part, *o_ref.shape[1:])


def fine_kernel(layout, u_ref, s_ref, st_ref, tis_ref, rt_ref, l_ref, o_ref, c_ref):
    total = o_ref.shape[0]
    held = layout.held
    group = math.gcd(total, 16)
    J = o_ref.shape[1] // SUBS
    own = s_ref.shape[2]
    o_ref[...] = (u_ref[:, 0] if len(u_ref.shape) == 5 else u_ref[...]).reshape(o_ref.shape)

    def step(_, carry):
        couple(o_ref, c_ref, st_ref, layout, rt_ref, l_ref)

        def turn(g, carry):
            at = (pl.ds(g * group, group),)
            q, c, tis = (rows_of(ref, at, J) for ref in (o_ref, c_ref, tis_ref))
            flat = lambda parts: [x.reshape(q[0].shape) for x in parts]
            n = group // held
            sto, per, lea = (
                flat(rows_of(st_ref, (pl.ds(g * n, n), slice(k * held, (k + 1) * held)), J)) for k in range(3)
            )
            n = group // own
            s = flat(rows_of(s_ref, (pl.ds(g * n, n), 1, slice(None)), J))
            put_rows(o_ref, at, J, implicit(q, s, c, sto, per, lea, tis, fine_size, SWEEPS))
            return carry

        return lax.fori_loop(0, total // group, turn, carry)

    lax.fori_loop(0, FINE_STEPS, step, 0)


def chain_kernel(layout, kind, *refs):
    if kind == 0:
        p_ref, field_ref, s_ref, u_ref = refs
    elif kind == 1:
        p_ref, field_ref, s_ref, f_ref, old_ref, u_ref, g_ref = refs
    else:
        p_ref, field_ref, s_ref, f_ref, old_ref, out_ref, u_ref = refs
    slices, own = s_ref.shape[:2]
    J = p_ref.shape[1] // SUBS
    held, inner = layout.held, layout.held // own
    x = lax.axis_index("x")
    all_own = slice(None)
    sto, per, lea = (rows_of(field_ref, (pl.ds(k * held + x * own, own),), J) for k in range(3))
    at = (lambda n: (n, 0, all_own)) if kind == 0 else (lambda n: (n, all_own))
    start = rows_of(p_ref, (pl.ds(x * own, own),), J)
    put_rows(u_ref, at(0), J, start)
    if kind == 0:
        u_ref[:, 1] = s_ref[...]

    def turn(n, u):
        s = rows_of(s_ref, (n, all_own), J)
        g = implicit(list(u), s, None, sto, per, lea, None, fine_size * FINE_STEPS, COARSE_SWEEPS)
        if kind:
            f = rows_of(f_ref, (n, all_own), J)
            old = rows_of(old_ref, (n + 1, 0, all_own) if len(old_ref.shape) == 5 else (n, all_own), J)
            if kind == 1:
                put_rows(g_ref, (n, all_own), J, g)
            g = [g[j] + (f[j] - old[j]) for j in range(J)]
        put_rows(u_ref, at(n + 1), J, g)
        return tuple(g)

    lax.fori_loop(0, slices - 1, turn, tuple(start))
    if kind == 1:
        g_ref[slices - 1] = jnp.zeros(g_ref.shape[1:], F32)
    if kind == 2:
        z = lax.axis_index("z")
        for k in range(inner):
            out_ref[k] = u_ref[z * inner + lax.rem(x + k, inner)]


def body(sizes, pressure0, storage, perm_base, leakoff, sources, export_cells, inter_local, trace_source, inter_trans, inter_count):
    groups, inner, fracs = sizes
    slices = groups * inner
    held, frac_rows, _ = pressure0.shape
    own = held // inner
    plane = ("frac", "x")
    layout = Layout(held, frac_rows, inter_local.size, export_cells.size)
    block = (own, frac_rows, LANES)

    blocks = jnp.broadcast_to(sources[0].reshape(1, inner, *block), (groups, inner, *block)).reshape(slices, *block)
    own_sources = lax.all_to_all(blocks, ("z", "x"), 0, 0, tiled=True)

    lists = [a.reshape(-1, LANES) for a in (inter_local, trace_source, inter_trans, export_cells)]
    (packed,) = call(
        functools.partial(pack_kernel, layout),
        "pack",
        (inter_count, storage, perm_base, leakoff, *lists, blocks),
        (shape_of(layout.slots, frac_rows, LANES),),
        [pltpu.VMEM(a.shape, a.dtype) for a in lists] + [pltpu.SemaphoreType.DMA((7,))],
        [SMEM] + [HBM] * 7 + [pl.BlockSpec(memory_space=pl.ANY)],
    )
    pieces = [packed] + [
        lax.ppermute(packed, "frac", [(i, (i + k) % fracs) for i in range(fracs)]) for k in range(1, fracs)
    ]
    own_sources, *pieces = lax.optimization_barrier((own_sources, *pieces))
    cells = held * frac_rows
    st, rt, l, tis = call(
        functools.partial(prep_kernel, layout),
        "prep",
        pieces,
        (
            shape_of(fracs, *packed.shape),
            shape_of(fracs, cells, inter_local.size, dtype=BF16),
            shape_of(fracs, inter_local.size, LANES, dtype=BF16),
            shape_of(fracs * held, frac_rows, LANES),
        ),
    )

    base = (pressure0, packed, own_sources)
    (u0,) = call(functools.partial(chain_kernel, layout, 0), "chain0", base, (shape_of(slices, 2, *block),))
    b0 = lax.all_to_all(u0, plane, 0, 0, tiled=True)
    u, old = b0, u0
    plain = shape_of(slices, *block)
    whole = (fracs * held, frac_rows, LANES)
    for iteration in range(ITERS):
        (ends,) = call(
            functools.partial(fine_kernel, layout),
            "fine",
            (u, b0, st, tis, rt, l),
            (shape_of(*whole),),
            [pltpu.VMEM(whole, F32)],
        )
        ends = lax.all_to_all(ends.reshape(plain.shape), plane, 0, 0, tiled=True)
        if iteration < ITERS - 1:
            states, old = call(functools.partial(chain_kernel, layout, 1), "chain1", (*base, ends, old), (plain, plain))
            u = lax.all_to_all(states, plane, 0, 0, tiled=True)
    (mine,) = call(
        functools.partial(chain_kernel, layout, 2),
        "chain2",
        (*base, ends, old),
        (shape_of(inner, *block),),
        [pltpu.VMEM(plain.shape, F32)],
    )
    x = lax.axis_index("x")
    got = [mine[0]] + [
        lax.ppermute(mine[k], "x", [(i, (i + k) % inner) for i in range(inner)]) for k in range(1, inner)
    ]
    return jnp.stack([lax.select_n((x - i) % inner, *got) if inner > 2 else jnp.where(x == i, got[0], got[-1]) for i in range(inner)]).reshape(1, held, frac_rows, LANES)


def solution(mesh):
    slices, fracs = mesh.shape["tm"], mesh.shape["frac"]
    inner = slices // fracs
    sizes = (slices // inner, inner, fracs)
    mesh = Mesh(mesh.devices.reshape(sizes), ("z", "x", "frac"))
    frac = P("frac")
    both = P(("z", "x"), "frac")
    return jax.shard_map(
        functools.partial(body, sizes),
        mesh=mesh,
        in_specs=(frac,) * 4 + (both,) + (frac,) * 5,
        out_specs=both,
        check_vma=False,
    )
```

time: 280 us -> 91.3 us (0.33)
  blocking collectives: 137 us -> 26.6 us
  other arithmetic: 80.9 us -> 0.64 us
  local copies, waits for them, and re-layouts: 56.4 us -> 7.13 us
  Pallas kernels: 0 us -> 24.2 us
  starting transfers between devices: 0 us -> 16.2 us
  waiting for transfers between devices: 0 us -> 15 us
  loops' own time: 3.94 us -> 0 us
    all_gather x11 -> x0, blocking collectives: 137 us -> none  [the longest x2 62.9 us: chain(): all_corrections = lax.all_gather(correction[None], 'tm', axis=0, tiled=True)]
    scatter-add x9 -> x0, other arithmetic: 53.5 us -> none  [the longest x8 47.6 us: couple(): return jnp.zeros_like(flat_field).at[inter_local].add(weights * remote_va...]
    gather x16 -> x0, local copies, waits for them, and re-layouts: 49.9 us -> none  [the longest x8 36.2 us: couple(): remote_values = gathered[trace_source]]
    all_to_all x0 -> x3, blocking collectives: none -> 26.6 us  [the longest x2 17.7 us: body(): ends = lax.all_to_all(ends.reshape(plain.shape), plane, 0, 0, tiled=True)]
    pallas_call x0 -> x7, Pallas kernels: none -> 24.2 us  [call(): pl.pallas_call(kernel, out_shape=outs, in_specs=specs or [VMEM] * len(arg...]
    all_to_all x0 -> x2, starting transfers between devices: none -> 12 us  [the longest x1 7.4 us: body(): own_sources = lax.all_to_all(blocks, ('z', 'x'), 0, 0, tiled=True)]
    ppermute x0 -> x4, waiting for transfers between devices: none -> 11 us  [the longest x3 8.16 us: body(): lax.ppermute(packed, 'frac', [(i, (i + k) % fracs) for i in range(fracs)])]
    slice x220 -> x0, other arithmetic: 10.5 us -> none  [the longest x110 8.95 us: next_cols(): array[:, :, 1:]]
  transfers between devices with their start and end apart: 0 -> 6, of which waited for: 0 -> 5; matrix products, arithmetic and copies ran while one was open for 0% -> 0% of each run, Pallas kernels for 0% -> 2%
where the time goes in v1:
time: 91.3 us; the launch traced here: 90.6 us
  blocking collectives  26.6 us (29%)
  Pallas kernels  24.2 us (27%)
  starting transfers between devices  16.2 us (18%)
  waiting for transfers between devices  15 us (16%)
  local copies, waits for them, and re-layouts  7.13 us (8%)
    pallas_call x7, Pallas kernels, call(): pl.pallas_call(kernel, out_shape=outs, in_specs=specs or [VMEM] * len(arg...  24.2 us
    all_to_all x2, blocking collectives, body(): ends = lax.all_to_all(ends.reshape(plain.shape), plane, 0, 0, tiled=True)  17.7 us
    all_to_all x1, blocking collectives, body(): u = lax.all_to_all(states, plane, 0, 0, tiled=True)  8.87 us
    ppermute x3, waiting for transfers between devices, body(): lax.ppermute(packed, 'frac', [(i, (i + k) % fracs) for i in range(fracs)])  8.16 us
    all_to_all x1, starting transfers between devices, body(): own_sources = lax.all_to_all(blocks, ('z', 'x'), 0, 0, tiled=True)  7.4 us
    unnamed x32, local copies, waits for them, and re-layouts  5.56 us
    all_to_all x1, starting transfers between devices, body(): b0 = lax.all_to_all(u0, plane, 0, 0, tiled=True)  4.65 us
    all_to_all x1, waiting for transfers between devices, body(): b0 = lax.all_to_all(u0, plane, 0, 0, tiled=True)  3.99 us
  transfers between devices with their start and end apart: 6, of which 5 were waited for; matrix products, arithmetic and copies ran while one was open for 0% of the time, Pallas kernels for 2%

profile of v1, /device:TPU:0, one launch (start us, length us, event | category | flops | bytes accessed | tf_op | source)
XLA Modules:
  0.0 90.6 jit_solution(2273389345847302288)
XLA Ops:
  0.0 1.6 %broadcast_in_dim.8 = f32[4,2,2,32,128]{4,3,2,1,0:T(8,128)} broadcast(f32[2,2,32,128]{3,2,1,0:T(8,128)} %bitcast.27), dimensions={1,2,3,4} | broadcast | bytes 327680 | tf_op jit(solution)/shard_map/broadcast_in_dim | solution.py:311
  1.6 0.0 copy-start.9
  1.6 0.0 copy-start.10
  1.6 0.0 copy-start.11
  1.6 0.0 copy-start.14
  1.6 7.4 %all-to-all-start = ((f32[8,2,32,128]{3,2,1,0:T(8,128)}), f32[8,2,32,128]{3,2,1,0:T(8,128)S(1)}, u32[]{:S(2)}, u32[]{:S(2)}) async-start(f32[8,2,32,128]{3,2,1,0:T(8,128)} %bitcast.5.blocks_ref), calls=%async_computation | async-start | bytes 524288 | tf_op jit(solution)/shard_map/all_to_all | solution.py:312
  9.0 0.0 copy-start.13
  9.6 0.0 copy-start.12
  9.7 0.0 copy-start.15
  9.7 0.0 copy-done.9
  9.7 0.0 copy-done.10
  9.7 0.0 copy-done.11
  9.7 0.0 copy-done.14
  9.7 0.0 copy-done.13
  9.7 0.6 copy-done.12
  10.3 0.0 copy-done.15
  10.3 0.0 copy-start.2
  10.3 0.3 pack.1.refs_1_.refs_0_
  10.7 0.1 collective-permute-start
  10.7 1.6 %collective-permute-start.1 = (f32[13,32,128]{2,1,0:T(8,128)S(1)}, f32[13,32,128]{2,1,0:T(8,128)S(1)}, u32[]{:S(2)}, u32[]{:S(2)}) collective-permute-start(f32[13,32,128]{2,1,0:T(8,128)S(1)} %pack.1.refs_1_.refs_0_), channel_id=1, source_target_pairs={{0,2},{1,3},{2,0},{3,1},{4,6},{5,7},{6,4},{7,5},{8,10},{9,11},{10,... | collective-permute-start | bytes 638984 | tf_op jit(solution)/shard_map/ppermute | solution.py:324
  12.3 1.4 %collective-permute-start.2 = (f32[13,32,128]{2,1,0:T(8,128)S(1)}, f32[13,32,128]{2,1,0:T(8,128)S(1)}, u32[]{:S(2)}, u32[]{:S(2)}) collective-permute-start(f32[13,32,128]{2,1,0:T(8,128)S(1)} %pack.1.refs_1_.refs_0_), channel_id=1, source_target_pairs={{0,3},{1,0},{2,1},{3,2},{4,7},{5,4},{6,5},{7,6},{8,11},{9,8},{10,9... | collective-permute-start | bytes 638984 | tf_op jit(solution)/shard_map/ppermute | solution.py:324
  13.7 4.0 %collective-permute-done.refs_1_ = f32[13,32,128]{2,1,0:T(8,128)S(1)} collective-permute-done((f32[13,32,128]{2,1,0:T(8,128)S(1)}, f32[13,32,128]{2,1,0:T(8,128)S(1)}, u32[]{:S(2)}, u32[]{:S(2)}) %collective-permute-start) | collective-permute-done | bytes 213024 | tf_op jit(solution)/shard_map/ppermute | solution.py:324
  17.7 0.0 copy-start.3
  17.7 1.2 %collective-permute-done.1.refs_2_ = f32[13,32,128]{2,1,0:T(8,128)S(1)} collective-permute-done((f32[13,32,128]{2,1,0:T(8,128)S(1)}, f32[13,32,128]{2,1,0:T(8,128)S(1)}, u32[]{:S(2)}, u32[]{:S(2)}) %collective-permute-start.1) | collective-permute-done | bytes 213024 | tf_op jit(solution)/shard_map/ppermute | solution.py:324
  18.9 0.0 copy-start.5
  18.9 3.0 %collective-permute-done.2.refs_3_ = f32[13,32,128]{2,1,0:T(8,128)S(1)} collective-permute-done((f32[13,32,128]{2,1,0:T(8,128)S(1)}, f32[13,32,128]{2,1,0:T(8,128)S(1)}, u32[]{:S(2)}, u32[]{:S(2)}) %collective-permute-start.2) | collective-permute-done | bytes 213024 | tf_op jit(solution)/shard_map/ppermute | solution.py:324
  21.9 0.0 copy-start.7
  21.9 0.0 all-to-all-done.refs_2_
  21.9 0.0 copy-done.2
  21.9 2.2 %chain0.1.refs_4_ = f32[8,2,2,32,128]{4,3,2,1,0:T(8,128)} custom-call(f32[4,32,128]{2,1,0:T(8,128)S(1)} %copy-done.2, f32[13,32,128]{2,1,0:T(8,128)S(1)} %pack.1.refs_1_.refs_0_, f32[8,2,32,128]{3,2,1,0:T(8,128)S(1)} %all-to-all-done.refs_2_), custom_call_target="tpu_custom_call" | custom-call | tf_op jit(solution)/shard_map/chain0/pallas_call | solution.py:35
  24.1 0.0 copy-done.3
  24.1 0.0 copy-done.5
  24.1 0.0 copy-done.7
  24.1 4.7 %all-to-all-start.1 = ((f32[8,2,2,32,128]{4,3,2,1,0:T(8,128)}), f32[8,2,2,32,128]{4,3,2,1,0:T(8,128)S(1)}, u32[]{:S(2)}, u32[]{:S(2)}) async-start(f32[8,2,2,32,128]{4,3,2,1,0:T(8,128)} %chain0.1.refs_4_), calls=%async_computation.1 | async-start | bytes 1048576 | tf_op jit(solution)/shard_map/all_to_all | solution.py:342
  28.7 0.0 copy-start.4
  28.7 0.9 %copy-done.4 = f32[13,32,128]{2,1,0:T(8,128)S(1)} copy-done((f32[13,32,128]{2,1,0:T(8,128)S(1)}, f32[13,32,128]{2,1,0:T(8,128)}, u32[]{:S(2)}) %copy-start.4) | copy-done | bytes 213016
  29.6 0.0 copy-start.6
  29.6 0.9 %copy-done.6 = f32[13,32,128]{2,1,0:T(8,128)S(1)} copy-done((f32[13,32,128]{2,1,0:T(8,128)S(1)}, f32[13,32,128]{2,1,0:T(8,128)}, u32[]{:S(2)}) %copy-start.6) | copy-done | bytes 213016
  30.6 0.0 copy-start.8
  30.6 0.9 %copy-done.8 = f32[13,32,128]{2,1,0:T(8,128)S(1)} copy-done((f32[13,32,128]{2,1,0:T(8,128)S(1)}, f32[13,32,128]{2,1,0:T(8,128)}, u32[]{:S(2)}) %copy-start.8) | copy-done | bytes 213016
  31.5 1.5 %prep.1 = (f32[4,13,32,128]{3,2,1,0:T(8,128)S(1)}, bf16[4,128,1024]{2,1,0:T(8,128)(2,1)S(1)}, bf16[4,1024,128]{2,1,0:T(8,128)(2,1)S(1)}, f32[16,32,128]{2,1,0:T(8,128)S(1)}) custom-call(f32[13,32,128]{2,1,0:T(8,128)S(1)} %pack.1.refs_1_.refs_0_, f32[13,32,128]{2,1,0:T(8,128)S(1)} %copy-done.4, f32[13,32,128]{2,1,0:T(8,128)S(1)} %copy-done.6, ...), custom_call_target="tpu_custom_call" | custom-call | tf_op jit(solution)/shard_map/prep/pallas_call | solution.py:35
  33.0 0.0 copy-start
  33.0 0.9 %copy-done = f32[4,13,32,128]{3,2,1,0:T(8,128)} copy-done((f32[4,13,32,128]{3,2,1,0:T(8,128)}, f32[4,13,32,128]{3,2,1,0:T(8,128)S(1)}, u32[]{:S(2)}) %copy-start) | copy-done | bytes 851992
  34.0 4.0 %all-to-all-done.1.u_ref.s_ref = f32[8,2,2,32,128]{4,3,2,1,0:T(8,128)S(1)} async-done(((f32[8,2,2,32,128]{4,3,2,1,0:T(8,128)}), f32[8,2,2,32,128]{4,3,2,1,0:T(8,128)S(1)}, u32[]{:S(2)}, u32[]{:S(2)}) %all-to-all-start.1) | async-done | bytes 524320 | tf_op jit(solution)/shard_map/all_to_all | solution.py:342
  38.0 0.0 copy-start.1
  38.0 1.2 %copy-done.1 = f32[4,13,32,128]{3,2,1,0:T(8,128)S(1)} copy-done((f32[4,13,32,128]{3,2,1,0:T(8,128)S(1)}, f32[4,13,32,128]{3,2,1,0:T(8,128)}, u32[]{:S(2)}) %copy-start.1) | copy-done | bytes 851992
  39.1 8.2 %fine.2 = f32[16,32,128]{2,1,0:T(8,128)S(1)} custom-call(f32[8,2,2,32,128]{4,3,2,1,0:T(8,128)S(1)} %all-to-all-done.1.u_ref.s_ref, f32[8,2,2,32,128]{4,3,2,1,0:T(8,128)S(1)} %all-to-all-done.1.u_ref.s_ref, f32[4,13,32,128]{3,2,1,0:T(8,128)S(1)} %copy-done.1, f32[16,32,128]{2,1,0:T(8,128)S(1)} %get-tuple-element.22.tis_ref, ...), custom_call_target="tpu_custom_call" | custom-call | tf_op jit(solution)/shard_map/fine/pallas_call | solution.py:35
  47.4 8.9 %all_to_all.25.refs_3_ = f32[8,2,32,128]{3,2,1,0:T(8,128)S(1)} all-to-all(f32[8,2,32,128]{3,2,1,0:T(8,128)S(1)} %bitcast.22), channel_id=1, replica_groups=mesh['z'=4,'x'=2,'frac'=4] {'frac','x'}, dimensions={0} | all-to-all | bytes 524288 | tf_op jit(solution)/shard_map/all_to_all | solution.py:354
  56.2 2.4 %chain1.1 = (f32[8,2,32,128]{3,2,1,0:T(8,128)S(1)}, f32[8,2,32,128]{3,2,1,0:T(8,128)S(1)}) custom-call(f32[4,32,128]{2,1,0:T(8,128)S(1)} %copy-done.2, f32[13,32,128]{2,1,0:T(8,128)S(1)} %pack.1.refs_1_.refs_0_, f32[8,2,32,128]{3,2,1,0:T(8,128)S(1)} %all-to-all-done.refs_2_, f32[8,2,32,128]{3,2,1,0:T(8,128)S(1)} %all_to_all.25.refs_3_, ...), custom_call_target="tpu_custom_call" | custom-call | tf_op jit(solution)/shard_map/chain1/pallas_call | solution.py:35
  58.6 8.9 %all_to_all.26.u_ref = f32[8,2,32,128]{3,2,1,0:T(8,128)S(1)} all-to-all(f32[8,2,32,128]{3,2,1,0:T(8,128)S(1)} %get-tuple-element.25), channel_id=1, replica_groups=mesh['z'=4,'x'=2,'frac'=4] {'frac','x'}, dimensions={0} | all-to-all | bytes 524288 | tf_op jit(solution)/shard_map/all_to_all | solution.py:357
  67.5 8.2 %fine.3 = f32[16,32,128]{2,1,0:T(8,128)S(1)} custom-call(f32[8,2,32,128]{3,2,1,0:T(8,128)S(1)} %all_to_all.26.u_ref, f32[8,2,2,32,128]{4,3,2,1,0:T(8,128)S(1)} %all-to-all-done.1.u_ref.s_ref, f32[4,13,32,128]{3,2,1,0:T(8,128)S(1)} %copy-done.1, f32[16,32,128]{2,1,0:T(8,128)S(1)} %get-tuple-element.22.tis_ref, ...), custom_call_target="tpu_custom_call" | custom-call | tf_op jit(solution)/shard_map/fine/pallas_call | solution.py:35
  75.8 8.9 %all_to_all.27.refs_3_ = f32[8,2,32,128]{3,2,1,0:T(8,128)S(1)} all-to-all(f32[8,2,32,128]{3,2,1,0:T(8,128)S(1)} %bitcast.21), channel_id=1, replica_groups=mesh['z'=4,'x'=2,'frac'=4] {'frac','x'}, dimensions={0} | all-to-all | bytes 524288 | tf_op jit(solution)/shard_map/all_to_all | solution.py:354
  84.6 1.4 %chain2.1 = f32[2,2,32,128]{3,2,1,0:T(8,128)S(1)} custom-call(f32[4,32,128]{2,1,0:T(8,128)S(1)} %copy-done.2, f32[13,32,128]{2,1,0:T(8,128)S(1)} %pack.1.refs_1_.refs_0_, f32[8,2,32,128]{3,2,1,0:T(8,128)S(1)} %all-to-all-done.refs_2_, f32[8,2,32,128]{3,2,1,0:T(8,128)S(1)} %all_to_all.27.refs_3_, f32[8,2,32,128]{3,2,1,0:T(8,128)S(1)} %get-tuple-element.26.refs_4_), custom_call_target="tpu_custom_call" | custom-call | tf_op jit(solution)/shard_map/chain2/pallas_call | solution.py:35
  86.0 1.1 %collective-permute-start.3 = (f32[2,32,128]{2,1,0:T(8,128)S(1)}, f32[2,32,128]{2,1,0:T(8,128)S(1)}, u32[]{:S(2)}, u32[]{:S(2)}) collective-permute-start(f32[2,32,128]{2,1,0:T(8,128)S(1)} %slice_bitcast_fusion), channel_id=1, source_target_pairs={{0,4},{4,0},{1,5},{5,1},{2,6},{6,2},{3,7},{7,3},{8,12},{12,8},{9,1... | collective-permute-start | bytes 98312 | tf_op jit(solution)/shard_map/ppermute | solution.py:367
  87.1 2.9 %collective-permute-done.3 = f32[2,32,128]{2,1,0:T(8,128)S(1)} collective-permute-done((f32[2,32,128]{2,1,0:T(8,128)S(1)}, f32[2,32,128]{2,1,0:T(8,128)S(1)}, u32[]{:S(2)}, u32[]{:S(2)}) %collective-permute-start.3) | collective-permute-done | bytes 32800 | tf_op jit(solution)/shard_map/ppermute | solution.py:367
  90.0 0.6 pad_maximum_fusion
  (2 shorter events, 0.0 us)
Async XLA Ops:
  1.6 8.1 %copy-start.9 = (f32[4,32,128]{2,1,0:T(8,128)S(1)}, f32[4,32,128]{2,1,0:T(8,128)}, u32[]{:S(2)}) copy-start(f32[4,32,128]{2,1,0:T(8,128)} %sto.1) | copy-start | bytes 196612
  1.6 8.1 %copy-start.10 = (f32[4,32,128]{2,1,0:T(8,128)S(1)}, f32[4,32,128]{2,1,0:T(8,128)}, u32[]{:S(2)}) copy-start(f32[4,32,128]{2,1,0:T(8,128)} %per.1) | copy-start | bytes 196612
  1.6 8.1 %copy-start.11 = (f32[4,32,128]{2,1,0:T(8,128)S(1)}, f32[4,32,128]{2,1,0:T(8,128)}, u32[]{:S(2)}) copy-start(f32[4,32,128]{2,1,0:T(8,128)} %lea.1) | copy-start | bytes 196612
  1.6 8.1 %copy-start.14 = (f32[1024]{0:T(1024)S(1)}, f32[1024]{0:T(1024)}, u32[]{:S(2)}) copy-start(f32[1024]{0:T(1024)} %param.18) | copy-start | bytes 12292
  1.6 20.3 %all-to-all-start = ((f32[8,2,32,128]{3,2,1,0:T(8,128)}), f32[8,2,32,128]{3,2,1,0:T(8,128)S(1)}, u32[]{:S(2)}, u32[]{:S(2)}) async-start(f32[8,2,32,128]{3,2,1,0:T(8,128)} %bitcast.5.blocks_ref), calls=%async_computation | async-start | bytes 524288 | tf_op jit(solution)/shard_map/all_to_all | solution.py:312
  9.0 0.7 copy-start.13
  9.6 0.7 copy-start.12
  9.7 0.7 copy-start.15
  10.3 11.6 %copy-start.2 = (f32[4,32,128]{2,1,0:T(8,128)S(1)}, f32[4,32,128]{2,1,0:T(8,128)}, u32[]{:S(2)}) copy-start(f32[4,32,128]{2,1,0:T(8,128)} %refs_0_.5) | copy-start | bytes 196612
  10.7 7.0 %collective-permute-start = (f32[13,32,128]{2,1,0:T(8,128)S(1)}, f32[13,32,128]{2,1,0:T(8,128)S(1)}, u32[]{:S(2)}, u32[]{:S(2)}) collective-permute-start(f32[13,32,128]{2,1,0:T(8,128)S(1)} %pack.1.refs_1_.refs_0_), channel_id=1, source_target_pairs={{0,1},{1,2},{2,3},{3,0},{4,5},{5,6},{6,7},{7,4},{8,9},{9,10},{10,1... | collective-permute-start | bytes 638984 | tf_op jit(solution)/shard_map/ppermute | solution.py:324
  10.7 8.1 %collective-permute-start.1 = (f32[13,32,128]{2,1,0:T(8,128)S(1)}, f32[13,32,128]{2,1,0:T(8,128)S(1)}, u32[]{:S(2)}, u32[]{:S(2)}) collective-permute-start(f32[13,32,128]{2,1,0:T(8,128)S(1)} %pack.1.refs_1_.refs_0_), channel_id=1, source_target_pairs={{0,2},{1,3},{2,0},{3,1},{4,6},{5,7},{6,4},{7,5},{8,10},{9,11},{10,... | collective-permute-start | bytes 638984 | tf_op jit(solution)/shard_map/ppermute | solution.py:324
  12.3 9.6 %collective-permute-start.2 = (f32[13,32,128]{2,1,0:T(8,128)S(1)}, f32[13,32,128]{2,1,0:T(8,128)S(1)}, u32[]{:S(2)}, u32[]{:S(2)}) collective-permute-start(f32[13,32,128]{2,1,0:T(8,128)S(1)} %pack.1.refs_1_.refs_0_), channel_id=1, source_target_pairs={{0,3},{1,0},{2,1},{3,2},{4,7},{5,4},{6,5},{7,6},{8,11},{9,8},{10,9... | collective-permute-start | bytes 638984 | tf_op jit(solution)/shard_map/ppermute | solution.py:324
  17.7 6.4 %copy-start.3 = (f32[13,32,128]{2,1,0:T(8,128)}, f32[13,32,128]{2,1,0:T(8,128)S(1)}, u32[]{:S(2)}) copy-start(f32[13,32,128]{2,1,0:T(8,128)S(1)} %collective-permute-done.refs_1_) | copy-start | bytes 638980
  18.9 5.2 %copy-start.5 = (f32[13,32,128]{2,1,0:T(8,128)}, f32[13,32,128]{2,1,0:T(8,128)S(1)}, u32[]{:S(2)}) copy-start(f32[13,32,128]{2,1,0:T(8,128)S(1)} %collective-permute-done.1.refs_2_) | copy-start | bytes 638980
  21.9 2.2 %copy-start.7 = (f32[13,32,128]{2,1,0:T(8,128)}, f32[13,32,128]{2,1,0:T(8,128)S(1)}, u32[]{:S(2)}) copy-start(f32[13,32,128]{2,1,0:T(8,128)S(1)} %collective-permute-done.2.refs_3_) | copy-start | bytes 638980
  24.1 13.9 %all-to-all-start.1 = ((f32[8,2,2,32,128]{4,3,2,1,0:T(8,128)}), f32[8,2,2,32,128]{4,3,2,1,0:T(8,128)S(1)}, u32[]{:S(2)}, u32[]{:S(2)}) async-start(f32[8,2,2,32,128]{4,3,2,1,0:T(8,128)} %chain0.1.refs_4_), calls=%async_computation.1 | async-start | bytes 1048576 | tf_op jit(solution)/shard_map/all_to_all | solution.py:342
  28.7 0.9 %copy-start.4 = (f32[13,32,128]{2,1,0:T(8,128)S(1)}, f32[13,32,128]{2,1,0:T(8,128)}, u32[]{:S(2)}) copy-start(f32[13,32,128]{2,1,0:T(8,128)} %copy-done.3) | copy-start | bytes 638980
  29.6 0.9 %copy-start.6 = (f32[13,32,128]{2,1,0:T(8,128)S(1)}, f32[13,32,128]{2,1,0:T(8,128)}, u32[]{:S(2)}) copy-start(f32[13,32,128]{2,1,0:T(8,128)} %copy-done.5) | copy-start | bytes 638980
  30.6 0.9 %copy-start.8 = (f32[13,32,128]{2,1,0:T(8,128)S(1)}, f32[13,32,128]{2,1,0:T(8,128)}, u32[]{:S(2)}) copy-start(f32[13,32,128]{2,1,0:T(8,128)} %copy-done.7) | copy-start | bytes 638980
  33.0 1.0 %copy-start = (f32[4,13,32,128]{3,2,1,0:T(8,128)}, f32[4,13,32,128]{3,2,1,0:T(8,128)S(1)}, u32[]{:S(2)}) copy-start(f32[4,13,32,128]{3,2,1,0:T(8,128)S(1)} %get-tuple-element.21.st_ref) | copy-start | bytes 2555908
  38.0 1.2 %copy-start.1 = (f32[4,13,32,128]{3,2,1,0:T(8,128)S(1)}, f32[4,13,32,128]{3,2,1,0:T(8,128)}, u32[]{:S(2)}) copy-start(f32[4,13,32,128]{3,2,1,0:T(8,128)} %copy-done) | copy-start | bytes 2555908
  86.0 4.0 %collective-permute-start.3 = (f32[2,32,128]{2,1,0:T(8,128)S(1)}, f32[2,32,128]{2,1,0:T(8,128)S(1)}, u32[]{:S(2)}, u32[]{:S(2)}) collective-permute-start(f32[2,32,128]{2,1,0:T(8,128)S(1)} %slice_bitcast_fusion), channel_id=1, source_target_pairs={{0,4},{4,0},{1,5},{5,1},{2,6},{6,2},{3,7},{7,3},{8,12},{12,8},{9,1... | collective-permute-start | bytes 98312 | tf_op jit(solution)/shard_map/ppermute | solution.py:367

commit v2 on v1

v2 whole, which is shorter than its diff:
```python
import functools
import math

import jax
import jax.numpy as jnp
from jax import lax
from jax.experimental import pallas as pl
from jax.experimental.pallas import tpu as pltpu
from jax.sharding import Mesh, PartitionSpec as P

FINE_STEPS = 4
SWEEPS = 8
COARSE_SWEEPS = 2
ITERS = 2

stress_factor = 0.15
fine_size = 0.25

LANES = 128
SUBS = 8
F32 = jnp.float32
BF16 = jnp.bfloat16
VMEM = pl.BlockSpec(memory_space=pltpu.VMEM)
HBM = pl.BlockSpec(memory_space=pltpu.HBM)


def shape_of(*dims, dtype=F32):
    return jax.ShapeDtypeStruct(dims, dtype)


def call(kernel, name, args, outs, scratch=(), specs=None, room=4 * 2**20):
    size = sum(math.prod(a.shape) * a.dtype.itemsize for a in (*args, *outs))
    return pl.pallas_call(
        kernel,
        out_shape=outs,
        in_specs=specs or [VMEM] * len(args),
        out_specs=(VMEM,) * len(outs),
        scratch_shapes=scratch,
        compiler_params=pltpu.CompilerParams(vmem_limit_bytes=room + size),
        name=name,
    )(*args)


def lane_roll(x, s):
    return pltpu.roll(x, s % LANES, axis=2)


def sub_roll(x, s):
    return pltpu.roll(x, s % SUBS, axis=1)


def columns_after(v):
    return v[1:] + [[lane_roll(x, -1) for x in v[0]]]


def columns_before(v):
    return [[lane_roll(x, 1) for x in v[-1]]] + v[:-1]


def rows_after(v):
    return [part[1:] + [sub_roll(part[0], -1)] for part in v]


def rows_before(v):
    return [[sub_roll(part[-1], 1)] + part[:-1] for part in v]


def implicit(q, s, c, sto, per, lea, tis, step_size, sweeps):
    M, J = len(q), len(q[0])
    shape = q[0][0].shape
    row = lax.broadcasted_iota(jnp.int32, shape, 1)
    col = lax.broadcasted_iota(jnp.int32, shape, 2) % (LANES // M)
    grid = [(k, j) for k in range(M) for j in range(J)]

    def each(f):
        return [[f(k, j) for j in range(J)] for k in range(M)]

    half = each(lambda k, j: (0.5 * per[k][j]) * jnp.exp(stress_factor * q[k][j]))
    down, up, right, left = rows_after(half), rows_before(half), columns_after(half), columns_before(half)
    row_next = each(lambda k, j: half[k][j] + down[k][j])
    row_prev = each(lambda k, j: half[k][j] + up[k][j] if j == 0 else row_next[k][j - 1])
    col_next = each(lambda k, j: half[k][j] + right[k][j])
    col_prev = each(lambda k, j: half[k][j] + left[k][j] if k == 0 else col_next[k - 1][j])
    for k in range(M):
        row_next[k][J - 1] = jnp.where(row == SUBS - 1, 0.0, row_next[k][J - 1])
        row_prev[k][0] = jnp.where(row == 0, 0.0, row_prev[k][0])
    for j in range(J):
        col_next[M - 1][j] = jnp.where(col == LANES // M - 1, 0.0, col_next[M - 1][j])
        col_prev[0][j] = jnp.where(col == 0, 0.0, col_prev[0][j])
    rhs, a_rn, a_rp, a_cn, a_cp = (each(lambda k, j: None) for _ in range(5))
    for k, j in grid:
        rate = sto[k][j] * (1.0 / step_size)
        total = rate + lea[k][j]
        b = rate * q[k][j] + s[k][j]
        if tis is not None:
            total = total + tis[k][j]
            b = b + c[k][j]
        inv = 1.0 / ((total + (row_next[k][j] + row_prev[k][j])) + (col_next[k][j] + col_prev[k][j]))
        rhs[k][j] = b * inv
        a_rn[k][j] = row_next[k][j] * inv
        a_rp[k][j] = row_prev[k][j] * inv
        a_cn[k][j] = col_next[k][j] * inv
        a_cp[k][j] = col_prev[k][j] * inv
    v = q
    for _ in range(sweeps):
        down, up, right, left = rows_after(v), rows_before(v), columns_after(v), columns_before(v)
        v = each(
            lambda k, j: (rhs[k][j] + a_rn[k][j] * down[k][j] + a_rp[k][j] * up[k][j])
            + (a_cn[k][j] * right[k][j] + a_cp[k][j] * left[k][j])
        )
    return v


def parts_of(ref, index, first, M, J):
    return [[ref[(*index, first + k, pl.ds(j * SUBS, SUBS), slice(None))] for j in range(J)] for k in range(M)]


def put_parts(ref, index, first, parts):
    for k, part in enumerate(parts):
        for j, x in enumerate(part):
            ref[(*index, first + k, pl.ds(j * SUBS, SUBS), slice(None))] = x


def pick_lanes(x, index):
    return jnp.take_along_axis(x, index, axis=1, mode="promise_in_bounds")


def to_parts(ref, first, M, J):
    lane = lax.broadcasted_iota(jnp.int32, (SUBS, LANES), 1)
    width = LANES // M
    out = [[None] * J for _ in range(M)]
    for j in range(J):
        rows = [ref[first + f, pl.ds(j, SUBS, stride=J), :] for f in range(M)]
        for k in range(M):
            x = pick_lanes(rows[0], lane % width * M + k)
            for f in range(1, M):
                x = jnp.where(lane // width == f, pick_lanes(rows[f], lane % width * M + k), x)
            out[k][j] = x
    return out


def from_parts(ref, index, parts):
    lane = lax.broadcasted_iota(jnp.int32, (SUBS, LANES), 1)
    M, J = len(parts), len(parts[0])
    width = LANES // M
    for j in range(J):
        for f in range(M):
            x = pick_lanes(parts[0][j], lane // M + f * width)
            for k in range(1, M):
                x = jnp.where(lane % M == k, pick_lanes(parts[k][j], lane // M + f * width), x)
            ref[(*index, f, pl.ds(j, SUBS, stride=J), slice(None))] = x


def split_high_low(x, pieces):
    out = []
    for _ in range(pieces):
        part = x.astype(BF16).astype(F32)
        out.append(part)
        x = x - part
    return out


def scatter_rows(values, rt_ref, l_ref, d):
    rows, entries = rt_ref.shape[1:]
    pieces = []
    for value in values:
        cols = []
        for m in range(entries // LANES):
            row = jnp.broadcast_to(value[m : m + 1, :], (2 * SUBS, LANES)).astype(BF16)
            hot = rt_ref[d, :, m * LANES : (m + 1) * LANES].reshape(-1, 2 * SUBS, LANES)
            cols.append((hot * row[None]).reshape(rows, LANES))
        pieces.append(jnp.concatenate(cols, axis=1))
    both = jnp.dot(jnp.concatenate(pieces, axis=0), l_ref[d], preferred_element_type=F32)
    out = both[:rows]
    for i in range(1, len(values)):
        out = out + both[i * rows : (i + 1) * rows]
    return jnp.concatenate([out[:, h * LANES : (h + 1) * LANES] for h in range(out.shape[1] // LANES)], axis=0)


class Layout:
    def __init__(self, held, own, pair, frac_rows, entries, exports):
        self.held, self.own, self.pair, self.frac_rows = held, own, pair, frac_rows
        self.J = frac_rows // SUBS
        self.entry_rows = entries // LANES
        self.export_rows = exports // LANES
        padded = -(-self.export_rows // SUBS) * SUBS
        self.sizes = [self.entry_rows] * 3 + [self.export_rows]
        self.slots = 3 * held + -(-(3 * self.entry_rows + padded) // frac_rows)

    def place(self, cell):
        own, J = self.own, self.J
        f, row, col = cell // (self.frac_rows * LANES), cell // LANES % self.frac_rows, cell % LANES
        part = (f // own * own + col % own) * J + row % J
        return (part * SUBS + row // J) * LANES + f % own * (LANES // own) + col // own

    def entries(self, ref, d, kind):
        start = kind * self.entry_rows
        return ref[d, start : start + self.sizes[kind], :]

    def put(self, ref, kind, value):
        at, left, start = 0, self.sizes[kind], kind * self.entry_rows
        while left:
            n = min(left, SUBS)
            slot, r = 3 * self.held + start // self.frac_rows, start % self.frac_rows
            ref[slot, r : r + n, :] = value[at : at + n]
            at, start, left = at + n, start + n, left - n


def pack_kernel(layout, *refs):
    sources = refs[:10]
    out_ref, blocks_ref, p_ref = refs[10:13]
    held_refs, sems = refs[13:23], refs[23]
    held, own, J = layout.held, layout.own, layout.J
    copies = [pltpu.make_async_copy(a, b, sems.at[k]) for k, (a, b) in enumerate(zip(sources, held_refs))]
    for c in copies:
        c.start()
    out_ref[3 * held :] = jnp.zeros((layout.slots - 3 * held, *out_ref.shape[1:]), F32)
    for c in copies:
        c.wait()
    *fields, p, source, loc, trace, w, exp, count_ref = held_refs
    for first in range(0, held, own):
        for k, field in enumerate(fields):
            put_parts(out_ref, (), k * held + first, to_parts(field, first, own, J))
        put_parts(p_ref, (), first, to_parts(p, first, own, J))
        parts = to_parts(source.at[0], first, own, J)
        for z in range(blocks_ref.shape[0]):
            put_parts(blocks_ref, (z,), first, parts)
    shape = w.shape
    index = lax.broadcasted_iota(jnp.int32, shape, 0) * LANES + lax.broadcasted_iota(jnp.int32, shape, 1)
    layout.put(out_ref, 0, layout.place(loc[...]).astype(F32))
    layout.put(out_ref, 1, trace[...].astype(F32))
    layout.put(out_ref, 2, jnp.where(index < count_ref[0], w[...], 0.0))
    layout.put(out_ref, 3, layout.place(exp[...]).astype(F32))


def hot_rows(layout, ent_ref, rt_ref):
    parts, rows, entries = rt_ref.shape
    iota = lax.broadcasted_iota(jnp.int32, (rows, LANES), 0)
    for d in range(parts):
        row = layout.entries(ent_ref, d, 0).astype(jnp.int32) // LANES % rows
        for m in range(entries // LANES):
            at = slice(m * LANES, (m + 1) * LANES)
            rt_ref[d, :, at] = jnp.where(iota == row[m : m + 1, :], 1.0, 0.0).astype(BF16)


def prep_kernel(layout, *refs):
    *piece_refs, fld_ref, ent_ref, l_ref, rt_ref = refs
    parts, rows, entries = rt_ref.shape
    held, own = layout.held, layout.own
    inner = held // own
    far, near = lax.axis_index("fo"), lax.axis_index("fi")
    pair = len(piece_refs)
    outer = parts // pair
    for i in range(pair):
        for o in range(outer):
            d = lax.rem(far - o + outer, outer) * pair + lax.rem(near - i + pair, pair)
            for k in range(3):
                for x in range(inner):
                    at = k * held + x * own
                    fld_ref[k, d * inner + x] = piece_refs[i][o, at : at + own]
            for slot in range(layout.slots - 3 * held):
                at = slot * layout.frac_rows
                ent_ref[d, at : at + layout.frac_rows, :] = piece_refs[i][o, 3 * held + slot]
    hot_rows(layout, ent_ref, rt_ref)
    for d in range(parts):
        cell = layout.entries(ent_ref, d, 0).astype(jnp.int32)
        col, half = cell % LANES, cell // LANES // rows
        for m in range(entries // LANES):
            at = slice(m * LANES, (m + 1) * LANES)
            iota_l = lax.broadcasted_iota(jnp.int32, (LANES, LANES), 0)
            for h in range(l_ref.shape[2] // LANES):
                mine = (iota_l == col[m : m + 1, :]) & (half[m : m + 1, :] == h)
                l_ref[d, at, h * LANES : (h + 1) * LANES] = jnp.where(mine, 1.0, 0.0).T.astype(BF16)
        tis = scatter_rows(split_high_low(layout.entries(ent_ref, d, 2), 3), rt_ref, l_ref, d)
        fld_ref[3, d * inner : (d + 1) * inner] = tis.reshape(inner, *fld_ref.shape[2:])


def couple(o_ref, c_ref, ent_ref, layout, rt_ref, l_ref):
    parts = rt_ref.shape[0]
    frac_rows, own = layout.frac_rows, layout.own
    inner = layout.held // own
    rows = layout.held * frac_rows
    export_rows = layout.export_rows
    iota = lax.broadcasted_iota(jnp.int32, (SUBS, LANES), 0)
    exported = []
    for d in range(parts):
        cell = layout.entries(ent_ref, d, 3).astype(jnp.int32)
        for e in range(export_rows):
            at = jnp.broadcast_to(cell[e : e + 1, :], (SUBS, LANES))
            row, col = at // LANES - iota, at % LANES
            found = [jnp.zeros((SUBS, LANES), F32) for _ in range(2)]
            for t in range(rows // SUBS):
                slot, r = t * SUBS // frac_rows, t * SUBS % frac_rows
                got = pick_lanes(o_ref[d * inner + slot // own, slot % own, r : r + SUBS, :], col)
                found[t % 2] = jnp.where(row == t * SUBS, got, found[t % 2])
            exported.append(jnp.sum(found[0] + found[1], axis=0, keepdims=True))
    for d in range(parts):
        slot = layout.entries(ent_ref, d, 1).astype(jnp.int32)
        row, col = slot // LANES, slot % LANES
        x = jnp.zeros(slot.shape, F32)
        for t in range(parts * export_rows):
            if t // export_rows != d:
                got = pick_lanes(jnp.broadcast_to(exported[t], slot.shape), col)
                x = jnp.where(row == t, got, x)
        c = scatter_rows(split_high_low(layout.entries(ent_ref, d, 2) * x, 2), rt_ref, l_ref, d)
        c_ref[d * inner : (d + 1) * inner] = c.reshape(inner, *o_ref.shape[1:])


def fine_kernel(layout, u_ref, s_ref, fld_ref, ent_ref, l_ref, o_ref, c_ref, rt_ref):
    total = o_ref.shape[0]
    own, J = layout.own, layout.J
    group = math.gcd(total, 8)
    hot_rows(layout, ent_ref, rt_ref)
    o_ref[...] = u_ref[:, 0] if len(u_ref.shape) == 5 else u_ref[...]

    def step(_, carry):
        couple(o_ref, c_ref, ent_ref, layout, rt_ref, l_ref)

        def turn(g, carry):
            at = pl.ds(g * group, group)
            q, c = (parts_of(ref, (at,), 0, own, J) for ref in (o_ref, c_ref))
            sto, per, lea, tis = (parts_of(fld_ref, (k, at), 0, own, J) for k in range(4))
            s = parts_of(s_ref, (at, 1), 0, own, J)
            put_parts(o_ref, (at,), 0, implicit(q, s, c, sto, per, lea, tis, fine_size, SWEEPS))
            return carry

        return lax.fori_loop(0, total // group, turn, carry)

    lax.fori_loop(0, FINE_STEPS, step, 0)


def chain_kernel(layout, kind, *refs):
    if kind == 0:
        p_ref, field_ref, s_ref, u_ref = refs
    elif kind == 1:
        p_ref, field_ref, s_ref, f_ref, old_ref, u_ref, g_ref = refs
    else:
        p_ref, field_ref, s_ref, f_ref, old_ref, out_ref, u_ref = refs
    slices = s_ref.shape[0]
    held, own, J = layout.held, layout.own, layout.J
    inner = held // own
    x = lax.axis_index("x")

    def parts(ref, *index, first=0):
        return [[y[None] for y in part] for part in parts_of(ref, index, first, own, J)]

    def put(ref, index, value):
        put_parts(ref, index, 0, [[y[0] for y in part] for part in value])

    mine = (lax.axis_index("fo") * layout.pair + lax.axis_index("fi")) * inner + x
    sto, per, lea = (parts(field_ref, k, mine) for k in range(3))
    at = (lambda n: (n, 0)) if kind == 0 else (lambda n: (n,))
    start = parts(p_ref, first=x * own)
    put(u_ref, at(0), start)
    if kind == 0:
        u_ref[:, 1] = s_ref[...]

    def turn(n, u):
        g = implicit(u, parts(s_ref, n), None, sto, per, lea, None, fine_size * FINE_STEPS, COARSE_SWEEPS)
        if kind:
            f = parts(f_ref, n)
            old = parts(old_ref, n + 1, 0) if len(old_ref.shape) == 5 else parts(old_ref, n)
            if kind == 1:
                put(g_ref, (n,), g)
            g = [[g[k][j] + (f[k][j] - old[k][j]) for j in range(J)] for k in range(own)]
        put(u_ref, at(n + 1), g)
        return g

    lax.fori_loop(0, slices - 1, turn, start)
    if kind == 1:
        g_ref[slices - 1] = jnp.zeros(g_ref.shape[1:], F32)
    if kind == 2:
        z = lax.axis_index("z")
        for k in range(inner):
            n = z * inner + lax.rem(x + k, inner)
            from_parts(out_ref, (k,), parts_of(u_ref, (n,), 0, own, J))


def gather_from(axis, a):
    n = lax.axis_size(axis)
    return [a] + [lax.ppermute(a, axis, [(i, (i + k) % n) for i in range(n)]) for k in range(1, n)]


def body(sizes, pressure0, storage, perm_base, leakoff, sources, export_cells, inter_local, trace_source, inter_trans, inter_count):
    groups, inner, outer, pair = sizes
    fracs = outer * pair
    slices = groups * inner
    held, frac_rows, _ = pressure0.shape
    own = held // inner
    plane = ("fo", "fi", "x")
    layout = Layout(held, own, pair, frac_rows, inter_local.size, export_cells.size)
    block = (own, frac_rows, LANES)
    plain = shape_of(slices, *block)

    lists = [a.reshape(-1, LANES) for a in (inter_local, trace_source, inter_trans, export_cells)]
    arrays = (storage, perm_base, leakoff, pressure0, sources, *lists, inter_count)
    packed, blocks, start = call(
        functools.partial(pack_kernel, layout),
        "pack",
        arrays,
        (shape_of(layout.slots, frac_rows, LANES), shape_of(groups, *pressure0.shape), shape_of(*pressure0.shape)),
        [pltpu.VMEM(a.shape, a.dtype) for a in arrays[:-1]]
        + [pltpu.SMEM(inter_count.shape, jnp.int32), pltpu.SemaphoreType.DMA((len(arrays),))],
        [HBM] * len(arrays),
        56 * 2**20,
    )
    far = gather_from("fo", packed[None])
    own_sources = lax.all_to_all(blocks.reshape(plain.shape), ("z", "x"), 0, 0, tiled=True)
    pieces = gather_from("fi", jnp.concatenate(far, axis=0))
    hot = pltpu.VMEM((fracs, held * frac_rows // 2, inter_local.size), BF16)
    fld, ent, l = call(
        functools.partial(prep_kernel, layout),
        "prep",
        pieces,
        (
            shape_of(4, slices, *block),
            shape_of(fracs, (layout.slots - 3 * held) * frac_rows, LANES),
            shape_of(fracs, inter_local.size, 2 * LANES, dtype=BF16),
        ),
        [hot],
    )
    own_sources, fld, ent, l = lax.optimization_barrier((own_sources, fld, ent, l))

    base = (start, fld, own_sources)
    (u0,) = call(functools.partial(chain_kernel, layout, 0), "chain0", base, (shape_of(slices, 2, *block),))
    b0 = lax.all_to_all(u0, plane, 0, 0, tiled=True)
    u, old = b0, u0
    for iteration in range(ITERS):
        (ends,) = call(
            functools.partial(fine_kernel, layout),
            "fine",
            (u, b0, fld, ent, l),
            (plain,),
            [pltpu.VMEM(plain.shape, F32), hot],
        )
        ends = lax.all_to_all(ends, plane, 0, 0, tiled=True)
        if iteration < ITERS - 1:
            states, old = call(functools.partial(chain_kernel, layout, 1), "chain1", (*base, ends, old), (plain, plain))
            u = lax.all_to_all(states, plane, 0, 0, tiled=True)
    (mine,) = call(
        functools.partial(chain_kernel, layout, 2),
        "chain2",
        (*base, ends, old),
        (shape_of(inner, *block),),
        [pltpu.VMEM(plain.shape, F32)],
    )
    x = lax.axis_index("x")
    got = [mine[0]] + [
        lax.ppermute(mine[k], "x", [(i, (i + k) % inner) for i in range(inner)]) for k in range(1, inner)
    ]
    return jnp.stack([lax.select_n((x - i) % inner, *got) if inner > 2 else jnp.where(x == i, got[0], got[-1]) for i in range(inner)]).reshape(1, held, frac_rows, LANES)


def solution(mesh):
    slices, fracs = mesh.shape["tm"], mesh.shape["frac"]
    inner = slices // fracs
    pair = math.gcd(fracs, 2)
    sizes = (slices // inner, inner, fracs // pair, pair)
    mesh = Mesh(mesh.devices.reshape(sizes), ("z", "x", "fo", "fi"))
    frac = P(("fo", "fi"))
    both = P(("z", "x"), ("fo", "fi"))
    return jax.shard_map(
        functools.partial(body, sizes),
        mesh=mesh,
        in_specs=(frac,) * 4 + (both,) + (frac,) * 5,
        out_specs=both,
        check_vma=False,
    )
```

time: 91.3 us -> 80.9 us (0.89)
  blocking collectives: 26.6 us -> 38.4 us
  local copies, waits for them, and re-layouts: 7.13 us -> 0.01 us
  starting transfers between devices: 16.2 us -> 10 us
  waiting for transfers between devices: 15 us -> 9.03 us
  Pallas kernels: 24.2 us -> 20.7 us
  other arithmetic: 0.64 us -> 1.6 us
    all_to_all x2 -> x3, blocking collectives: 17.7 us -> 29.5 us  [the longest x2 17.7 us: body(): ends = lax.all_to_all(ends, plane, 0, 0, tiled=True)]
    ppermute x3 -> x2, waiting for transfers between devices: 8.16 us -> 1.76 us  [gather_from(): lax.ppermute(a, axis, [(i, (i + k) % n) for i in range(n)])]
    all_to_all x2 -> x1, starting transfers between devices: 12 us -> 5.81 us  [body(): lax.all_to_all(blocks.reshape(plain.shape), ('z', 'x'), 0, 0, tiled=True)]
    unnamed x32 -> x2, local copies, waits for them, and re-layouts: 5.56 us -> 0.01 us
    pallas_call x7, Pallas kernels: 24.2 us -> 20.7 us  [call(): pl.pallas_call(kernel, out_shape=outs, in_specs=specs or [VMEM] * len(arg...]
    broadcast_in_dim x1 -> x0, local copies, waits for them, and re-layouts: 1.57 us -> none  [body(): jnp.broadcast_to(sources[0].reshape(1, inner, *block), (groups, inner, *b...]
    concatenate x0 -> x1, other arithmetic: none -> 0.96 us  [body(): pieces = gather_from('fi', jnp.concatenate(far, axis=0))]
    all_to_all x2 -> x1, waiting for transfers between devices: 4 us -> 4.4 us  [body(): lax.all_to_all(blocks.reshape(plain.shape), ('z', 'x'), 0, 0, tiled=True)]
  transfers between devices with their start and end apart: 6 -> 4, of which waited for: 5 -> 3; matrix products, arithmetic and copies ran while one was open for 0% -> 1% of each run, Pallas kernels for 2% -> 2%
where the time goes in v2:
time: 80.9 us; the launch traced here: 80.5 us
  blocking collectives  38.4 us (47%)
  Pallas kernels  20.7 us (26%)
  starting transfers between devices  10 us (12%)
  waiting for transfers between devices  9.03 us (11%)
  other arithmetic  1.6 us (2%)
    pallas_call x7, Pallas kernels, call(): pl.pallas_call(kernel, out_shape=outs, in_specs=specs or [VMEM] * len(arg...  20.7 us
    all_to_all x2, blocking collectives, body(): ends = lax.all_to_all(ends, plane, 0, 0, tiled=True)  17.7 us
    all_to_all x1, blocking collectives, body(): b0 = lax.all_to_all(u0, plane, 0, 0, tiled=True)  11.8 us
    all_to_all x1, blocking collectives, body(): u = lax.all_to_all(states, plane, 0, 0, tiled=True)  8.87 us
    all_to_all x1, starting transfers between devices, body(): lax.all_to_all(blocks.reshape(plain.shape), ('z', 'x'), 0, 0, tiled=True)  5.81 us
    all_to_all x1, waiting for transfers between devices, body(): lax.all_to_all(blocks.reshape(plain.shape), ('z', 'x'), 0, 0, tiled=True)  4.4 us
    ppermute x2, starting transfers between devices, gather_from(): lax.ppermute(a, axis, [(i, (i + k) % n) for i in range(n)])  3.1 us
    ppermute x1, waiting for transfers between devices, body(): lax.ppermute(mine[k], 'x', [(i, (i + k) % inner) for i in range(inner)])  2.87 us
  transfers between devices with their start and end apart: 4, of which 3 were waited for; matrix products, arithmetic and copies ran while one was open for 1% of the time, Pallas kernels for 2%

profile of v2, /device:TPU:0, one launch (start us, length us, event | category | flops | bytes accessed | tf_op | source)
XLA Modules:
  0.0 80.5 jit_solution(5733244144448887942)
XLA Ops:
  0.7 2.2 %pack.1 = (f32[13,32,128]{2,1,0:T(8,128)}, f32[4,4,32,128]{3,2,1,0:T(8,128)}, f32[4,32,128]{2,1,0:T(8,128)}) custom-call(f32[4,32,128]{2,1,0:T(8,128)} %refs_0_.1, f32[4,32,128]{2,1,0:T(8,128)} %refs_1_.1, f32[4,32,128]{2,1,0:T(8,128)} %refs_2_.1, f32[4,32,128]{2,1,0:T(8,128)} %refs_3_.1, f32[1,4,32,128]{3,2,1,0:T(8,128)} %refs_4_.1, s32[8,128]{1,0:T(8,128)} %bitcast.22, ...), custom_call_target="tpu_custom_call" | custom-call | tf_op jit(solution)/shard_map/pack/pallas_call | solution.py:33
  2.9 0.0 copy-start
  2.9 3.0 %collective-permute-start = (f32[1,13,32,128]{3,2,1,0:T(8,128)}, f32[1,13,32,128]{3,2,1,0:T(8,128)S(1)}, u32[]{:S(2)}, u32[]{:S(2)}) collective-permute-start(f32[1,13,32,128]{3,2,1,0:T(8,128)} %bitcast.20), channel_id=1, source_target_pairs={{0,2},{2,0},{1,3},{3,1},{4,6},{6,4},{5,7},{7,5},{8,10},{10,8},{9,1... | collective-permute-start | bytes 638984 | tf_op jit(solution)/shard_map/ppermute | solution.py:381
  5.9 5.8 %all-to-all-start = ((f32[8,2,32,128]{3,2,1,0:T(8,128)}), f32[8,2,32,128]{3,2,1,0:T(8,128)S(1)}, u32[]{:S(2)}, u32[]{:S(2)}) async-start(f32[8,2,32,128]{3,2,1,0:T(8,128)} %bitcast.19), calls=%async_computation | async-start | bytes 524288 | tf_op jit(solution)/shard_map/all_to_all | solution.py:408
  11.7 0.0 collective-permute-done
  11.7 1.0 %pad_maximum_fusion.refs_0_ = f32[2,13,32,128]{3,2,1,0:T(8,128)S(1)} fusion(f32[1,13,32,128]{3,2,1,0:T(8,128)S(1)} %collective-permute-done, f32[1,13,32,128]{3,2,1,0:T(8,128)} %bitcast.21), kind=kLoop, calls=%fused_computation | loop fusion | flops 106496 | bytes 851968 | tf_op jit(solution)/shard_map/concatenate | solution.py:409
  12.7 0.1 collective-permute-start.1
  12.8 1.8 %collective-permute-done.1.refs_1_ = f32[2,13,32,128]{3,2,1,0:T(8,128)S(1)} collective-permute-done((f32[2,13,32,128]{3,2,1,0:T(8,128)S(1)}, f32[2,13,32,128]{3,2,1,0:T(8,128)S(1)}, u32[]{:S(2)}, u32[]{:S(2)}) %collective-permute-start.1) | collective-permute-done | bytes 426016 | tf_op jit(solution)/shard_map/ppermute | solution.py:381
  14.6 1.4 %prep.1 = (f32[4,8,2,32,128]{4,3,2,1,0:T(8,128)S(1)}, f32[4,32,128]{2,1,0:T(8,128)S(1)}, bf16[4,1024,256]{2,1,0:T(8,128)(2,1)S(1)}) custom-call(f32[2,13,32,128]{3,2,1,0:T(8,128)S(1)} %pad_maximum_fusion.refs_0_, f32[2,13,32,128]{3,2,1,0:T(8,128)S(1)} %collective-permute-done.1.refs_1_), custom_call_target="tpu_custom_call" | custom-call | tf_op jit(solution)/shard_map/prep/pallas_call | solution.py:33
  16.0 4.4 %all-to-all-done.refs_2_ = f32[8,2,32,128]{3,2,1,0:T(8,128)S(1)} async-done(((f32[8,2,32,128]{3,2,1,0:T(8,128)}), f32[8,2,32,128]{3,2,1,0:T(8,128)S(1)}, u32[]{:S(2)}, u32[]{:S(2)}) %all-to-all-start) | async-done | bytes 262176 | tf_op jit(solution)/shard_map/all_to_all | solution.py:408
  20.4 0.0 copy-done
  20.4 1.3 %chain0.1.refs_4_ = f32[8,2,2,32,128]{4,3,2,1,0:T(8,128)S(1)} custom-call(f32[4,32,128]{2,1,0:T(8,128)S(1)} %copy-done, f32[4,8,2,32,128]{4,3,2,1,0:T(8,128)S(1)} %get-tuple-element.23.refs_1_.fld_ref, f32[8,2,32,128]{3,2,1,0:T(8,128)S(1)} %all-to-all-done.refs_2_), custom_call_target="tpu_custom_call" | custom-call | tf_op jit(solution)/shard_map/chain0/pallas_call | solution.py:33
  21.7 11.8 %all_to_all.25.u_ref.s_ref = f32[8,2,2,32,128]{4,3,2,1,0:T(8,128)S(1)} all-to-all(f32[8,2,2,32,128]{4,3,2,1,0:T(8,128)S(1)} %chain0.1.refs_4_), channel_id=1, replica_groups=mesh['z'=4,'x'=2,'fo'=2,'fi'=2] {'fo','fi','x'}, dimensions={0} | all-to-all | bytes 1048576 | tf_op jit(solution)/shard_map/all_to_all | solution.py:426
  33.5 6.5 %fine.2 = f32[8,2,32,128]{3,2,1,0:T(8,128)S(1)} custom-call(f32[8,2,2,32,128]{4,3,2,1,0:T(8,128)S(1)} %all_to_all.25.u_ref.s_ref, f32[8,2,2,32,128]{4,3,2,1,0:T(8,128)S(1)} %all_to_all.25.u_ref.s_ref, f32[4,8,2,32,128]{4,3,2,1,0:T(8,128)S(1)} %get-tuple-element.23.refs_1_.fld_ref, f32[4,32,128]{2,1,0:T(8,128)S(1)} %get-tuple-element.25.ent_ref, ...), custom_call_target="tpu_custom_call" | custom-call | tf_op jit(solution)/shard_map/fine/pallas_call | solution.py:33
  40.0 8.9 %all_to_all.26.refs_3_ = f32[8,2,32,128]{3,2,1,0:T(8,128)S(1)} all-to-all(f32[8,2,32,128]{3,2,1,0:T(8,128)S(1)} %fine.2), channel_id=1, replica_groups=mesh['z'=4,'x'=2,'fo'=2,'fi'=2] {'fo','fi','x'}, dimensions={0} | all-to-all | bytes 524288 | tf_op jit(solution)/shard_map/all_to_all | solution.py:436
  48.9 1.3 %chain1.1 = (f32[8,2,32,128]{3,2,1,0:T(8,128)S(1)}, f32[8,2,32,128]{3,2,1,0:T(8,128)S(1)}) custom-call(f32[4,32,128]{2,1,0:T(8,128)S(1)} %copy-done, f32[4,8,2,32,128]{4,3,2,1,0:T(8,128)S(1)} %get-tuple-element.23.refs_1_.fld_ref, f32[8,2,32,128]{3,2,1,0:T(8,128)S(1)} %all-to-all-done.refs_2_, f32[8,2,32,128]{3,2,1,0:T(8,128)S(1)} %all_to_all.26.refs_3_, ...), custom_call_target="tpu_custom_call" | custom-call | tf_op jit(solution)/shard_map/chain1/pallas_call | solution.py:33
  50.2 8.9 %all_to_all.27.u_ref = f32[8,2,32,128]{3,2,1,0:T(8,128)S(1)} all-to-all(f32[8,2,32,128]{3,2,1,0:T(8,128)S(1)} %get-tuple-element.27), channel_id=1, replica_groups=mesh['z'=4,'x'=2,'fo'=2,'fi'=2] {'fo','fi','x'}, dimensions={0} | all-to-all | bytes 524288 | tf_op jit(solution)/shard_map/all_to_all | solution.py:439
  59.0 6.5 %fine.3 = f32[8,2,32,128]{3,2,1,0:T(8,128)S(1)} custom-call(f32[8,2,32,128]{3,2,1,0:T(8,128)S(1)} %all_to_all.27.u_ref, f32[8,2,2,32,128]{4,3,2,1,0:T(8,128)S(1)} %all_to_all.25.u_ref.s_ref, f32[4,8,2,32,128]{4,3,2,1,0:T(8,128)S(1)} %get-tuple-element.23.refs_1_.fld_ref, f32[4,32,128]{2,1,0:T(8,128)S(1)} %get-tuple-element.25.ent_ref, ...), custom_call_target="tpu_custom_call" | custom-call | tf_op jit(solution)/shard_map/fine/pallas_call | solution.py:33
  65.6 8.9 %all_to_all.28.refs_3_ = f32[8,2,32,128]{3,2,1,0:T(8,128)S(1)} all-to-all(f32[8,2,32,128]{3,2,1,0:T(8,128)S(1)} %fine.3), channel_id=1, replica_groups=mesh['z'=4,'x'=2,'fo'=2,'fi'=2] {'fo','fi','x'}, dimensions={0} | all-to-all | bytes 524288 | tf_op jit(solution)/shard_map/all_to_all | solution.py:436
  74.4 1.4 %chain2.1 = f32[2,2,32,128]{3,2,1,0:T(8,128)S(1)} custom-call(f32[4,32,128]{2,1,0:T(8,128)S(1)} %copy-done, f32[4,8,2,32,128]{4,3,2,1,0:T(8,128)S(1)} %get-tuple-element.23.refs_1_.fld_ref, f32[8,2,32,128]{3,2,1,0:T(8,128)S(1)} %all-to-all-done.refs_2_, f32[8,2,32,128]{3,2,1,0:T(8,128)S(1)} %all_to_all.28.refs_3_, ...), custom_call_target="tpu_custom_call" | custom-call | tf_op jit(solution)/shard_map/chain2/pallas_call | solution.py:33
  75.9 1.1 %collective-permute-start.2 = (f32[2,32,128]{2,1,0:T(8,128)S(1)}, f32[2,32,128]{2,1,0:T(8,128)S(1)}, u32[]{:S(2)}, u32[]{:S(2)}) collective-permute-start(f32[2,32,128]{2,1,0:T(8,128)S(1)} %slice_bitcast_fusion), channel_id=1, source_target_pairs={{0,4},{4,0},{1,5},{5,1},{2,6},{6,2},{3,7},{7,3},{8,12},{12,8},{9,1... | collective-permute-start | bytes 98312 | tf_op jit(solution)/shard_map/ppermute | solution.py:449
  77.0 2.9 %collective-permute-done.2 = f32[2,32,128]{2,1,0:T(8,128)S(1)} collective-permute-done((f32[2,32,128]{2,1,0:T(8,128)S(1)}, f32[2,32,128]{2,1,0:T(8,128)S(1)}, u32[]{:S(2)}, u32[]{:S(2)}) %collective-permute-start.2) | collective-permute-done | bytes 32800 | tf_op jit(solution)/shard_map/ppermute | solution.py:449
  79.9 0.6 pad_maximum_fusion.1
  (2 shorter events, 0.0 us)
Async XLA Ops:
  2.9 17.5 %copy-start = (f32[4,32,128]{2,1,0:T(8,128)S(1)}, f32[4,32,128]{2,1,0:T(8,128)}, u32[]{:S(2)}) copy-start(f32[4,32,128]{2,1,0:T(8,128)} %get-tuple-element.17.refs_0_) | copy-start | bytes 196612
  2.9 8.8 %collective-permute-start = (f32[1,13,32,128]{3,2,1,0:T(8,128)}, f32[1,13,32,128]{3,2,1,0:T(8,128)S(1)}, u32[]{:S(2)}, u32[]{:S(2)}) collective-permute-start(f32[1,13,32,128]{3,2,1,0:T(8,128)} %bitcast.20), channel_id=1, source_target_pairs={{0,2},{2,0},{1,3},{3,1},{4,6},{6,4},{5,7},{7,5},{8,10},{10,8},{9,1... | collective-permute-start | bytes 638984 | tf_op jit(solution)/shard_map/ppermute | solution.py:381
  5.9 14.4 %all-to-all-start = ((f32[8,2,32,128]{3,2,1,0:T(8,128)}), f32[8,2,32,128]{3,2,1,0:T(8,128)S(1)}, u32[]{:S(2)}, u32[]{:S(2)}) async-start(f32[8,2,32,128]{3,2,1,0:T(8,128)} %bitcast.19), calls=%async_computation | async-start | bytes 524288 | tf_op jit(solution)/shard_map/all_to_all | solution.py:408
  12.7 1.8 %collective-permute-start.1 = (f32[2,13,32,128]{3,2,1,0:T(8,128)S(1)}, f32[2,13,32,128]{3,2,1,0:T(8,128)S(1)}, u32[]{:S(2)}, u32[]{:S(2)}) collective-permute-start(f32[2,13,32,128]{3,2,1,0:T(8,128)S(1)} %pad_maximum_fusion.refs_0_), channel_id=1, source_target_pairs={{0,1},{1,0},{2,3},{3,2},{4,5},{5,4},{6,7},{7,6},{8,9},{9,8},{10,11... | collective-permute-start | bytes 1277960 | tf_op jit(solution)/shard_map/ppermute | solution.py:381
  75.9 4.0 %collective-permute-start.2 = (f32[2,32,128]{2,1,0:T(8,128)S(1)}, f32[2,32,128]{2,1,0:T(8,128)S(1)}, u32[]{:S(2)}, u32[]{:S(2)}) collective-permute-start(f32[2,32,128]{2,1,0:T(8,128)S(1)} %slice_bitcast_fusion), channel_id=1, source_target_pairs={{0,4},{4,0},{1,5},{5,1},{2,6},{6,2},{3,7},{7,3},{8,12},{12,8},{9,1... | collective-permute-start | bytes 98312 | tf_op jit(solution)/shard_map/ppermute | solution.py:449

commit v3 on v2

--- a/solution.py
+++ b/solution.py
@@ -49,34 +49,17 @@
     return pltpu.roll(x, s % SUBS, axis=1)
 
 
-def columns_after(v):
-    return v[1:] + [[lane_roll(x, -1) for x in v[0]]]
-
-
-def columns_before(v):
-    return [[lane_roll(x, 1) for x in v[-1]]] + v[:-1]
-
-
-def rows_after(v):
-    return [part[1:] + [sub_roll(part[0], -1)] for part in v]
-
-
-def rows_before(v):
-    return [[sub_roll(part[-1], 1)] + part[:-1] for part in v]
-
-
-def implicit(q, s, c, sto, per, lea, tis, step_size, sweeps):
+def coefficients(q, sto, per, lea, tis, step_size):
     M, J = len(q), len(q[0])
     shape = q[0][0].shape
     row = lax.broadcasted_iota(jnp.int32, shape, 1)
     col = lax.broadcasted_iota(jnp.int32, shape, 2) % (LANES // M)
-    grid = [(k, j) for k in range(M) for j in range(J)]
 
     def each(f):
         return [[f(k, j) for j in range(J)] for k in range(M)]
 
     half = each(lambda k, j: (0.5 * per[k][j]) * jnp.exp(stress_factor * q[k][j]))
-    down, up, right, left = rows_after(half), rows_before(half), columns_after(half), columns_before(half)
+    down, up, right, left = neighbours(half, rolled(half))
     row_next = each(lambda k, j: half[k][j] + down[k][j])
     row_prev = each(lambda k, j: half[k][j] + up[k][j] if j == 0 else row_next[k][j - 1])
     col_next = each(lambda k, j: half[k][j] + right[k][j])
@@ -87,27 +70,62 @@
     for j in range(J):
         col_next[M - 1][j] = jnp.where(col == LANES // M - 1, 0.0, col_next[M - 1][j])
         col_prev[0][j] = jnp.where(col == 0, 0.0, col_prev[0][j])
-    rhs, a_rn, a_rp, a_cn, a_cp = (each(lambda k, j: None) for _ in range(5))
-    for k, j in grid:
-        rate = sto[k][j] * (1.0 / step_size)
-        total = rate + lea[k][j]
-        b = rate * q[k][j] + s[k][j]
+
+    def inverse(k, j):
+        total = sto[k][j] * (1.0 / step_size) + lea[k][j]
         if tis is not None:
             total = total + tis[k][j]
-            b = b + c[k][j]
-        inv = 1.0 / ((total + (row_next[k][j] + row_prev[k][j])) + (col_next[k][j] + col_prev[k][j]))
-        rhs[k][j] = b * inv
-        a_rn[k][j] = row_next[k][j] * inv
-        a_rp[k][j] = row_prev[k][j] * inv
-        a_cn[k][j] = col_next[k][j] * inv
-        a_cp[k][j] = col_prev[k][j] * inv
-    v = q
-    for _ in range(sweeps):
-        down, up, right, left = rows_after(v), rows_before(v), columns_after(v), columns_before(v)
-        v = each(
-            lambda k, j: (rhs[k][j] + a_rn[k][j] * down[k][j] + a_rp[k][j] * up[k][j])
-            + (a_cn[k][j] * right[k][j] + a_cp[k][j] * left[k][j])
-        )
+        return 1.0 / ((total + (row_next[k][j] + row_prev[k][j])) + (col_next[k][j] + col_prev[k][j]))
+
+    inv = each(inverse)
+    return [inv] + [each(lambda k, j: t[k][j] * inv[k][j]) for t in (row_next, row_prev, col_next, col_prev)]
+
+
+def rolled(v):
+    return (
+        [sub_roll(part[0], -1) for part in v],
+        [sub_roll(part[-1], 1) for part in v],
+        [lane_roll(x, -1) for x in v[0]],
+        [lane_roll(x, 1) for x in v[-1]],
+    )
+
+
+def neighbours(v, edges):
+    after, before, right, left = edges
+    return (
+        [part[1:] + [after[k]] for k, part in enumerate(v)],
+        [[before[k]] + part[:-1] for k, part in enumerate(v)],
+        v[1:] + [right],
+        [left] + v[:-1],
+    )
+
+
+def implicit(q, sto, per, lea, tis, sources, step_size, sweeps):
+    M, J = len(q[0]), len(q[0][0])
+    grid = [(k, j) for k in range(M) for j in range(J)]
+    blocks = range(len(q))
+    known, edges, rhs = [], [], []
+    for b in blocks:
+        s = sources(b)
+        known.append(coefficients(q[b], sto[b], per[b], lea[b], None if tis is None else tis[b], step_size))
+        edges.append(rolled(q[b]))
+        inv = known[b][0]
+        rhs.append([[None] * J for _ in range(M)])
+        for k, j in grid:
+            rhs[b][k][j] = (sto[b][k][j] * (1.0 / step_size) * q[b][k][j] + s[k][j]) * inv[k][j]
+    v = list(q)
+    for sweep in range(sweeps):
+        for b in blocks:
+            _, a_rn, a_rp, a_cn, a_cp = known[b]
+            down, up, right, left = neighbours(v[b], edges[b])
+            new = [[None] * J for _ in range(M)]
+            for k, j in grid:
+                new[k][j] = (rhs[b][k][j] + a_rn[k][j] * down[k][j] + a_rp[k][j] * up[k][j]) + (
+                    a_cn[k][j] * right[k][j] + a_cp[k][j] * left[k][j]
+                )
+            v[b] = new
+            if sweep < sweeps - 1:
+                edges[b] = rolled(new)
     return v
 
 
@@ -275,8 +293,7 @@
         fld_ref[3, d * inner : (d + 1) * inner] = tis.reshape(inner, *fld_ref.shape[2:])
 
 
-def couple(o_ref, c_ref, ent_ref, layout, rt_ref, l_ref):
-    parts = rt_ref.shape[0]
+def arriving(o_ref, ent_ref, layout, parts):
     frac_rows, own = layout.frac_rows, layout.own
     inner = layout.held // own
     rows = layout.held * frac_rows
@@ -294,6 +311,7 @@
                 got = pick_lanes(o_ref[d * inner + slot // own, slot % own, r : r + SUBS, :], col)
                 found[t % 2] = jnp.where(row == t * SUBS, got, found[t % 2])
             exported.append(jnp.sum(found[0] + found[1], axis=0, keepdims=True))
+    out = []
     for d in range(parts):
         slot = layout.entries(ent_ref, d, 1).astype(jnp.int32)
         row, col = slot // LANES, slot % LANES
@@ -302,8 +320,8 @@
             if t // export_rows != d:
                 got = pick_lanes(jnp.broadcast_to(exported[t], slot.shape), col)
                 x = jnp.where(row == t, got, x)
-        c = scatter_rows(split_high_low(layout.entries(ent_ref, d, 2) * x, 2), rt_ref, l_ref, d)
-        c_ref[d * inner : (d + 1) * inner] = c.reshape(inner, *o_ref.shape[1:])
+        out.append(layout.entries(ent_ref, d, 2) * x)
+    return out
 
 
 def fine_kernel(layout, u_ref, s_ref, fld_ref, ent_ref, l_ref, o_ref, c_ref, rt_ref):
@@ -313,23 +331,41 @@
     hot_rows(layout, ent_ref, rt_ref)
     o_ref[...] = u_ref[:, 0] if len(u_ref.shape) == 5 else u_ref[...]
 
+    fracs, inner = rt_ref.shape[0], layout.held // own
+
+    def couple(d, values):
+        c = scatter_rows(split_high_low(values, 2), rt_ref, l_ref, d)
+        c_ref[d * inner : (d + 1) * inner] = c.reshape(inner, *c_ref.shape[1:])
+
+    def one_step(first):
+        def blocks(ref, *index):
+            return [parts_of(ref, (*index, pl.ds(first + b, 1)), 0, own, J) for b in range(group)]
+
+        def sources(b):
+            c = parts_of(c_ref, (pl.ds(first + b, 1),), 0, own, J)
+            s = parts_of(s_ref, (pl.ds(first + b, 1), 1), 0, own, J)
+            return [[s[k][j] + c[k][j] for j in range(J)] for k in range(own)]
+
+        sto, per, lea, tis = (blocks(fld_ref, k) for k in range(4))
+        out = implicit(blocks(o_ref), sto, per, lea, tis, sources, fine_size, SWEEPS)
+        for b in range(group):
+            put_parts(o_ref, (pl.ds(first + b, 1),), 0, out[b])
+
     def step(_, carry):
-        couple(o_ref, c_ref, ent_ref, layout, rt_ref, l_ref)
+        values = arriving(o_ref, ent_ref, layout, fracs)
+        for d in range(fracs):
+            couple(d, values[d])
 
         def turn(g, carry):
-            at = pl.ds(g * group, group)
-            q, c = (parts_of(ref, (at,), 0, own, J) for ref in (o_ref, c_ref))
-            sto, per, lea, tis = (parts_of(fld_ref, (k, at), 0, own, J) for k in range(4))
-            s = parts_of(s_ref, (at, 1), 0, own, J)
-            put_parts(o_ref, (at,), 0, implicit(q, s, c, sto, per, lea, tis, fine_size, SWEEPS))
+            one_step(g * group)
             return carry
 
-        return lax.fori_loop(0, total // group, turn, carry)
+        return turn(0, carry) if total == group else lax.fori_loop(0, total // group, turn, carry)
 
     lax.fori_loop(0, FINE_STEPS, step, 0)
 
 
-def chain_kernel(layout, kind, *refs):
+def chain_kernel(layout, kind, done, *refs):
     if kind == 0:
         p_ref, field_ref, s_ref, u_ref = refs
     elif kind == 1:
@@ -356,7 +392,8 @@
         u_ref[:, 1] = s_ref[...]
 
     def turn(n, u):
-        g = implicit(u, parts(s_ref, n), None, sto, per, lea, None, fine_size * FINE_STEPS, COARSE_SWEEPS)
+        sources = lambda b: parts(s_ref, n)
+        (g,) = implicit([u], [sto], [per], [lea], None, sources, fine_size * FINE_STEPS, COARSE_SWEEPS)
         if kind:
             f = parts(f_ref, n)
             old = parts(old_ref, n + 1, 0) if len(old_ref.shape) == 5 else parts(old_ref, n)
@@ -366,7 +403,12 @@
         put(u_ref, at(n + 1), g)
         return g
 
-    lax.fori_loop(0, slices - 1, turn, start)
+    for n in range(done):
+        start = parts(f_ref, n)
+        put(u_ref, at(n + 1), start)
+        if kind == 1:
+            g_ref[n] = jnp.zeros(g_ref.shape[1:], F32)
+    lax.fori_loop(done, slices - 1, turn, start)
     if kind == 1:
         g_ref[slices - 1] = jnp.zeros(g_ref.shape[1:], F32)
     if kind == 2:
@@ -422,7 +464,7 @@
     own_sources, fld, ent, l = lax.optimization_barrier((own_sources, fld, ent, l))
 
     base = (start, fld, own_sources)
-    (u0,) = call(functools.partial(chain_kernel, layout, 0), "chain0", base, (shape_of(slices, 2, *block),))
+    (u0,) = call(functools.partial(chain_kernel, layout, 0, 0), "chain0", base, (shape_of(slices, 2, *block),))
     b0 = lax.all_to_all(u0, plane, 0, 0, tiled=True)
     u, old = b0, u0
     for iteration in range(ITERS):
@@ -435,10 +477,10 @@
         )
         ends = lax.all_to_all(ends, plane, 0, 0, tiled=True)
         if iteration < ITERS - 1:
-            states, old = call(functools.partial(chain_kernel, layout, 1), "chain1", (*base, ends, old), (plain, plain))
+            states, old = call(functools.partial(chain_kernel, layout, 1, iteration + 1), "chain1", (*base, ends, old), (plain, plain))
             u = lax.all_to_all(states, plane, 0, 0, tiled=True)
     (mine,) = call(
-        functools.partial(chain_kernel, layout, 2),
+        functools.partial(chain_kernel, layout, 2, ITERS),
         "chain2",
         (*base, ends, old),
         (shape_of(inner, *block),),

time: 80.9 us -> 80.3 us (level)
  no operation moved by 1% of the time
where the time goes in v3:
time: 80.3 us; the launch traced here: 79.8 us
  blocking collectives  38.4 us (48%)
  Pallas kernels  20 us (25%)
  starting transfers between devices  10 us (12%)
  waiting for transfers between devices  9.03 us (11%)
  other arithmetic  1.6 us (2%)
    pallas_call x7, Pallas kernels, call(): pl.pallas_call(kernel, out_shape=outs, in_specs=specs or [VMEM] * len(arg...  20 us
    all_to_all x2, blocking collectives, body(): ends = lax.all_to_all(ends, plane, 0, 0, tiled=True)  17.7 us
    all_to_all x1, blocking collectives, body(): b0 = lax.all_to_all(u0, plane, 0, 0, tiled=True)  11.8 us
    all_to_all x1, blocking collectives, body(): u = lax.all_to_all(states, plane, 0, 0, tiled=True)  8.87 us
    all_to_all x1, starting transfers between devices, body(): lax.all_to_all(blocks.reshape(plain.shape), ('z', 'x'), 0, 0, tiled=True)  5.81 us
    all_to_all x1, waiting for transfers between devices, body(): lax.all_to_all(blocks.reshape(plain.shape), ('z', 'x'), 0, 0, tiled=True)  4.4 us
    ppermute x2, starting transfers between devices, gather_from(): lax.ppermute(a, axis, [(i, (i + k) % n) for i in range(n)])  3.1 us
    ppermute x1, waiting for transfers between devices, body(): lax.ppermute(mine[k], 'x', [(i, (i + k) % inner) for i in range(inner)])  2.87 us
  transfers between devices with their start and end apart: 4, of which 3 were waited for; matrix products, arithmetic and copies ran while one was open for 1% of the time, Pallas kernels for 2%

profile of v3, /device:TPU:0, one launch (start us, length us, event | category | flops | bytes accessed | tf_op | source)
XLA Modules:
  0.0 79.8 jit_solution(12363118768213960016)
XLA Ops:
  0.7 2.2 %pack.1 = (f32[13,32,128]{2,1,0:T(8,128)}, f32[4,4,32,128]{3,2,1,0:T(8,128)}, f32[4,32,128]{2,1,0:T(8,128)}) custom-call(f32[4,32,128]{2,1,0:T(8,128)} %refs_0_.1, f32[4,32,128]{2,1,0:T(8,128)} %refs_1_.1, f32[4,32,128]{2,1,0:T(8,128)} %refs_2_.1, f32[4,32,128]{2,1,0:T(8,128)} %refs_3_.1, f32[1,4,32,128]{3,2,1,0:T(8,128)} %refs_4_.1, s32[8,128]{1,0:T(8,128)} %bitcast.22, ...), custom_call_target="tpu_custom_call" | custom-call | tf_op jit(solution)/shard_map/pack/pallas_call | solution.py:33
  2.9 0.0 copy-start
  2.9 3.0 %collective-permute-start = (f32[1,13,32,128]{3,2,1,0:T(8,128)}, f32[1,13,32,128]{3,2,1,0:T(8,128)S(1)}, u32[]{:S(2)}, u32[]{:S(2)}) collective-permute-start(f32[1,13,32,128]{3,2,1,0:T(8,128)} %bitcast.20), channel_id=1, source_target_pairs={{0,2},{2,0},{1,3},{3,1},{4,6},{6,4},{5,7},{7,5},{8,10},{10,8},{9,1... | collective-permute-start | bytes 638984 | tf_op jit(solution)/shard_map/ppermute | solution.py:423
  5.9 5.8 %all-to-all-start = ((f32[8,2,32,128]{3,2,1,0:T(8,128)}), f32[8,2,32,128]{3,2,1,0:T(8,128)S(1)}, u32[]{:S(2)}, u32[]{:S(2)}) async-start(f32[8,2,32,128]{3,2,1,0:T(8,128)} %bitcast.19), calls=%async_computation | async-start | bytes 524288 | tf_op jit(solution)/shard_map/all_to_all | solution.py:450
  11.7 0.0 collective-permute-done
  11.7 1.0 %pad_maximum_fusion.refs_0_ = f32[2,13,32,128]{3,2,1,0:T(8,128)S(1)} fusion(f32[1,13,32,128]{3,2,1,0:T(8,128)S(1)} %collective-permute-done, f32[1,13,32,128]{3,2,1,0:T(8,128)} %bitcast.21), kind=kLoop, calls=%fused_computation | loop fusion | flops 106496 | bytes 851968 | tf_op jit(solution)/shard_map/concatenate | solution.py:451
  12.7 0.1 collective-permute-start.1
  12.8 1.8 %collective-permute-done.1.refs_1_ = f32[2,13,32,128]{3,2,1,0:T(8,128)S(1)} collective-permute-done((f32[2,13,32,128]{3,2,1,0:T(8,128)S(1)}, f32[2,13,32,128]{3,2,1,0:T(8,128)S(1)}, u32[]{:S(2)}, u32[]{:S(2)}) %collective-permute-start.1) | collective-permute-done | bytes 426016 | tf_op jit(solution)/shard_map/ppermute | solution.py:423
  14.6 1.4 %prep.1 = (f32[4,8,2,32,128]{4,3,2,1,0:T(8,128)S(1)}, f32[4,32,128]{2,1,0:T(8,128)S(1)}, bf16[4,1024,256]{2,1,0:T(8,128)(2,1)S(1)}) custom-call(f32[2,13,32,128]{3,2,1,0:T(8,128)S(1)} %pad_maximum_fusion.refs_0_, f32[2,13,32,128]{3,2,1,0:T(8,128)S(1)} %collective-permute-done.1.refs_1_), custom_call_target="tpu_custom_call" | custom-call | tf_op jit(solution)/shard_map/prep/pallas_call | solution.py:33
  16.0 4.4 %all-to-all-done.refs_2_ = f32[8,2,32,128]{3,2,1,0:T(8,128)S(1)} async-done(((f32[8,2,32,128]{3,2,1,0:T(8,128)}), f32[8,2,32,128]{3,2,1,0:T(8,128)S(1)}, u32[]{:S(2)}, u32[]{:S(2)}) %all-to-all-start) | async-done | bytes 262176 | tf_op jit(solution)/shard_map/all_to_all | solution.py:450
  20.4 0.0 copy-done
  20.4 1.3 %chain0.1.refs_4_ = f32[8,2,2,32,128]{4,3,2,1,0:T(8,128)S(1)} custom-call(f32[4,32,128]{2,1,0:T(8,128)S(1)} %copy-done, f32[4,8,2,32,128]{4,3,2,1,0:T(8,128)S(1)} %get-tuple-element.23.refs_1_.fld_ref, f32[8,2,32,128]{3,2,1,0:T(8,128)S(1)} %all-to-all-done.refs_2_), custom_call_target="tpu_custom_call" | custom-call | tf_op jit(solution)/shard_map/chain0/pallas_call | solution.py:33
  21.7 11.8 %all_to_all.25.u_ref.s_ref = f32[8,2,2,32,128]{4,3,2,1,0:T(8,128)S(1)} all-to-all(f32[8,2,2,32,128]{4,3,2,1,0:T(8,128)S(1)} %chain0.1.refs_4_), channel_id=1, replica_groups=mesh['z'=4,'x'=2,'fo'=2,'fi'=2] {'fo','fi','x'}, dimensions={0} | all-to-all | bytes 1048576 | tf_op jit(solution)/shard_map/all_to_all | solution.py:468
  33.5 6.5 %fine.2 = f32[8,2,32,128]{3,2,1,0:T(8,128)S(1)} custom-call(f32[8,2,2,32,128]{4,3,2,1,0:T(8,128)S(1)} %all_to_all.25.u_ref.s_ref, f32[8,2,2,32,128]{4,3,2,1,0:T(8,128)S(1)} %all_to_all.25.u_ref.s_ref, f32[4,8,2,32,128]{4,3,2,1,0:T(8,128)S(1)} %get-tuple-element.23.refs_1_.fld_ref, f32[4,32,128]{2,1,0:T(8,128)S(1)} %get-tuple-element.25.ent_ref, ...), custom_call_target="tpu_custom_call" | custom-call | tf_op jit(solution)/shard_map/fine/pallas_call | solution.py:33
  40.0 8.9 %all_to_all.26.refs_3_ = f32[8,2,32,128]{3,2,1,0:T(8,128)S(1)} all-to-all(f32[8,2,32,128]{3,2,1,0:T(8,128)S(1)} %fine.2), channel_id=1, replica_groups=mesh['z'=4,'x'=2,'fo'=2,'fi'=2] {'fo','fi','x'}, dimensions={0} | all-to-all | bytes 524288 | tf_op jit(solution)/shard_map/all_to_all | solution.py:478
  48.8 1.1 %chain1.1 = (f32[8,2,32,128]{3,2,1,0:T(8,128)S(1)}, f32[8,2,32,128]{3,2,1,0:T(8,128)S(1)}) custom-call(f32[4,32,128]{2,1,0:T(8,128)S(1)} %copy-done, f32[4,8,2,32,128]{4,3,2,1,0:T(8,128)S(1)} %get-tuple-element.23.refs_1_.fld_ref, f32[8,2,32,128]{3,2,1,0:T(8,128)S(1)} %all-to-all-done.refs_2_, f32[8,2,32,128]{3,2,1,0:T(8,128)S(1)} %all_to_all.26.refs_3_, ...), custom_call_target="tpu_custom_call" | custom-call | tf_op jit(solution)/shard_map/chain1/pallas_call | solution.py:33
  49.9 8.9 %all_to_all.27.u_ref = f32[8,2,32,128]{3,2,1,0:T(8,128)S(1)} all-to-all(f32[8,2,32,128]{3,2,1,0:T(8,128)S(1)} %get-tuple-element.27), channel_id=1, replica_groups=mesh['z'=4,'x'=2,'fo'=2,'fi'=2] {'fo','fi','x'}, dimensions={0} | all-to-all | bytes 524288 | tf_op jit(solution)/shard_map/all_to_all | solution.py:481
  58.8 6.5 %fine.3 = f32[8,2,32,128]{3,2,1,0:T(8,128)S(1)} custom-call(f32[8,2,32,128]{3,2,1,0:T(8,128)S(1)} %all_to_all.27.u_ref, f32[8,2,2,32,128]{4,3,2,1,0:T(8,128)S(1)} %all_to_all.25.u_ref.s_ref, f32[4,8,2,32,128]{4,3,2,1,0:T(8,128)S(1)} %get-tuple-element.23.refs_1_.fld_ref, f32[4,32,128]{2,1,0:T(8,128)S(1)} %get-tuple-element.25.ent_ref, ...), custom_call_target="tpu_custom_call" | custom-call | tf_op jit(solution)/shard_map/fine/pallas_call | solution.py:33
  65.3 8.9 %all_to_all.28.refs_3_ = f32[8,2,32,128]{3,2,1,0:T(8,128)S(1)} all-to-all(f32[8,2,32,128]{3,2,1,0:T(8,128)S(1)} %fine.3), channel_id=1, replica_groups=mesh['z'=4,'x'=2,'fo'=2,'fi'=2] {'fo','fi','x'}, dimensions={0} | all-to-all | bytes 524288 | tf_op jit(solution)/shard_map/all_to_all | solution.py:478
  74.1 1.0 %chain2.1 = f32[2,2,32,128]{3,2,1,0:T(8,128)S(1)} custom-call(f32[4,32,128]{2,1,0:T(8,128)S(1)} %copy-done, f32[4,8,2,32,128]{4,3,2,1,0:T(8,128)S(1)} %get-tuple-element.23.refs_1_.fld_ref, f32[8,2,32,128]{3,2,1,0:T(8,128)S(1)} %all-to-all-done.refs_2_, f32[8,2,32,128]{3,2,1,0:T(8,128)S(1)} %all_to_all.28.refs_3_, ...), custom_call_target="tpu_custom_call" | custom-call | tf_op jit(solution)/shard_map/chain2/pallas_call | solution.py:33
  75.2 1.1 %collective-permute-start.2 = (f32[2,32,128]{2,1,0:T(8,128)S(1)}, f32[2,32,128]{2,1,0:T(8,128)S(1)}, u32[]{:S(2)}, u32[]{:S(2)}) collective-permute-start(f32[2,32,128]{2,1,0:T(8,128)S(1)} %slice_bitcast_fusion), channel_id=1, source_target_pairs={{0,4},{4,0},{1,5},{5,1},{2,6},{6,2},{3,7},{7,3},{8,12},{12,8},{9,1... | collective-permute-start | bytes 98312 | tf_op jit(solution)/shard_map/ppermute | solution.py:491
  76.3 2.9 %collective-permute-done.2 = f32[2,32,128]{2,1,0:T(8,128)S(1)} collective-permute-done((f32[2,32,128]{2,1,0:T(8,128)S(1)}, f32[2,32,128]{2,1,0:T(8,128)S(1)}, u32[]{:S(2)}, u32[]{:S(2)}) %collective-permute-start.2) | collective-permute-done | bytes 32800 | tf_op jit(solution)/shard_map/ppermute | solution.py:491
  79.2 0.6 pad_maximum_fusion.1
  (2 shorter events, 0.0 us)
Async XLA Ops:
  2.9 17.5 %copy-start = (f32[4,32,128]{2,1,0:T(8,128)S(1)}, f32[4,32,128]{2,1,0:T(8,128)}, u32[]{:S(2)}) copy-start(f32[4,32,128]{2,1,0:T(8,128)} %get-tuple-element.17.refs_0_) | copy-start | bytes 196612
  2.9 8.8 %collective-permute-start = (f32[1,13,32,128]{3,2,1,0:T(8,128)}, f32[1,13,32,128]{3,2,1,0:T(8,128)S(1)}, u32[]{:S(2)}, u32[]{:S(2)}) collective-permute-start(f32[1,13,32,128]{3,2,1,0:T(8,128)} %bitcast.20), channel_id=1, source_target_pairs={{0,2},{2,0},{1,3},{3,1},{4,6},{6,4},{5,7},{7,5},{8,10},{10,8},{9,1... | collective-permute-start | bytes 638984 | tf_op jit(solution)/shard_map/ppermute | solution.py:423
  5.9 14.4 %all-to-all-start = ((f32[8,2,32,128]{3,2,1,0:T(8,128)}), f32[8,2,32,128]{3,2,1,0:T(8,128)S(1)}, u32[]{:S(2)}, u32[]{:S(2)}) async-start(f32[8,2,32,128]{3,2,1,0:T(8,128)} %bitcast.19), calls=%async_computation | async-start | bytes 524288 | tf_op jit(solution)/shard_map/all_to_all | solution.py:450
  12.7 1.8 %collective-permute-start.1 = (f32[2,13,32,128]{3,2,1,0:T(8,128)S(1)}, f32[2,13,32,128]{3,2,1,0:T(8,128)S(1)}, u32[]{:S(2)}, u32[]{:S(2)}) collective-permute-start(f32[2,13,32,128]{3,2,1,0:T(8,128)S(1)} %pad_maximum_fusion.refs_0_), channel_id=1, source_target_pairs={{0,1},{1,0},{2,3},{3,2},{4,5},{5,4},{6,7},{7,6},{8,9},{9,8},{10,11... | collective-permute-start | bytes 1277960 | tf_op jit(solution)/shard_map/ppermute | solution.py:423
  75.2 4.0 %collective-permute-start.2 = (f32[2,32,128]{2,1,0:T(8,128)S(1)}, f32[2,32,128]{2,1,0:T(8,128)S(1)}, u32[]{:S(2)}, u32[]{:S(2)}) collective-permute-start(f32[2,32,128]{2,1,0:T(8,128)S(1)} %slice_bitcast_fusion), channel_id=1, source_target_pairs={{0,4},{4,0},{1,5},{5,1},{2,6},{6,2},{3,7},{7,3},{8,12},{12,8},{9,1... | collective-permute-start | bytes 98312 | tf_op jit(solution)/shard_map/ppermute | solution.py:491

commit v4 on v3

--- a/solution.py
+++ b/solution.py
@@ -241,8 +241,8 @@
             put_parts(out_ref, (), k * held + first, to_parts(field, first, own, J))
         put_parts(p_ref, (), first, to_parts(p, first, own, J))
         parts = to_parts(source.at[0], first, own, J)
-        for z in range(blocks_ref.shape[0]):
-            put_parts(blocks_ref, (z,), first, parts)
+        for z in range(blocks_ref.shape[1]):
+            put_parts(blocks_ref, (first // own, z), 0, parts)
     shape = w.shape
     index = lax.broadcasted_iota(jnp.int32, shape, 0) * LANES + lax.broadcasted_iota(jnp.int32, shape, 1)
     layout.put(out_ref, 0, layout.place(loc[...]).astype(F32))
@@ -275,7 +275,7 @@
             for k in range(3):
                 for x in range(inner):
                     at = k * held + x * own
-                    fld_ref[k, d * inner + x] = piece_refs[i][o, at : at + own]
+                    fld_ref[k, x * parts + d] = piece_refs[i][o, at : at + own]
             for slot in range(layout.slots - 3 * held):
                 at = slot * layout.frac_rows
                 ent_ref[d, at : at + layout.frac_rows, :] = piece_refs[i][o, 3 * held + slot]
@@ -290,7 +290,9 @@
                 mine = (iota_l == col[m : m + 1, :]) & (half[m : m + 1, :] == h)
                 l_ref[d, at, h * LANES : (h + 1) * LANES] = jnp.where(mine, 1.0, 0.0).T.astype(BF16)
         tis = scatter_rows(split_high_low(layout.entries(ent_ref, d, 2), 3), rt_ref, l_ref, d)
-        fld_ref[3, d * inner : (d + 1) * inner] = tis.reshape(inner, *fld_ref.shape[2:])
+        tis = tis.reshape(inner, *fld_ref.shape[2:])
+        for x in range(inner):
+            fld_ref[3, x * parts + d] = tis[x]
 
 
 def arriving(o_ref, ent_ref, layout, parts):
@@ -308,7 +310,7 @@
             found = [jnp.zeros((SUBS, LANES), F32) for _ in range(2)]
             for t in range(rows // SUBS):
                 slot, r = t * SUBS // frac_rows, t * SUBS % frac_rows
-                got = pick_lanes(o_ref[d * inner + slot // own, slot % own, r : r + SUBS, :], col)
+                got = pick_lanes(o_ref[slot // own * parts + d, slot % own, r : r + SUBS, :], col)
                 found[t % 2] = jnp.where(row == t * SUBS, got, found[t % 2])
             exported.append(jnp.sum(found[0] + found[1], axis=0, keepdims=True))
     out = []
@@ -335,7 +337,9 @@
 
     def couple(d, values):
         c = scatter_rows(split_high_low(values, 2), rt_ref, l_ref, d)
-        c_ref[d * inner : (d + 1) * inner] = c.reshape(inner, *c_ref.shape[1:])
+        c = c.reshape(inner, *c_ref.shape[1:])
+        for x in range(inner):
+            c_ref[x * fracs + d] = c[x]
 
     def one_step(first):
         def blocks(ref, *index):
@@ -377,22 +381,26 @@
     inner = held // own
     x = lax.axis_index("x")
 
+    def at_source(n):
+        return n % inner * (slices // inner) + n // inner
+
     def parts(ref, *index, first=0):
         return [[y[None] for y in part] for part in parts_of(ref, index, first, own, J)]
 
     def put(ref, index, value):
         put_parts(ref, index, 0, [[y[0] for y in part] for part in value])
 
-    mine = (lax.axis_index("fo") * layout.pair + lax.axis_index("fi")) * inner + x
+    mine = x * (slices // inner) + lax.axis_index("fo") * layout.pair + lax.axis_index("fi")
     sto, per, lea = (parts(field_ref, k, mine) for k in range(3))
     at = (lambda n: (n, 0)) if kind == 0 else (lambda n: (n,))
     start = parts(p_ref, first=x * own)
     put(u_ref, at(0), start)
     if kind == 0:
-        u_ref[:, 1] = s_ref[...]
+        for n in range(slices):
+            u_ref[n, 1] = s_ref[at_source(n)]
 
     def turn(n, u):
-        sources = lambda b: parts(s_ref, n)
+        sources = lambda b: parts(s_ref, at_source(n))
         (g,) = implicit([u], [sto], [per], [lea], None, sources, fine_size * FINE_STEPS, COARSE_SWEEPS)
         if kind:
             f = parts(f_ref, n)
@@ -429,7 +437,7 @@
     slices = groups * inner
     held, frac_rows, _ = pressure0.shape
     own = held // inner
-    plane = ("fo", "fi", "x")
+    plane = ("x", "fo", "fi")
     layout = Layout(held, own, pair, frac_rows, inter_local.size, export_cells.size)
     block = (own, frac_rows, LANES)
     plain = shape_of(slices, *block)
@@ -440,14 +448,14 @@
         functools.partial(pack_kernel, layout),
         "pack",
         arrays,
-        (shape_of(layout.slots, frac_rows, LANES), shape_of(groups, *pressure0.shape), shape_of(*pressure0.shape)),
+        (shape_of(layout.slots, frac_rows, LANES), shape_of(inner, groups, *block), shape_of(*pressure0.shape)),
         [pltpu.VMEM(a.shape, a.dtype) for a in arrays[:-1]]
         + [pltpu.SMEM(inter_count.shape, jnp.int32), pltpu.SemaphoreType.DMA((len(arrays),))],
         [HBM] * len(arrays),
         56 * 2**20,
     )
     far = gather_from("fo", packed[None])
-    own_sources = lax.all_to_all(blocks.reshape(plain.shape), ("z", "x"), 0, 0, tiled=True)
+    own_sources = lax.all_to_all(blocks.reshape(plain.shape), ("x", "z"), 0, 0, tiled=True)
     pieces = gather_from("fi", jnp.concatenate(far, axis=0))
     hot = pltpu.VMEM((fracs, held * frac_rows // 2, inter_local.size), BF16)
     fld, ent, l = call(

time: 80.3 us -> 80 us (level)
  blocking collectives: 38.4 us -> 37.2 us
    all_to_all x1, waiting for transfers between devices: 4.4 us -> 5.44 us  [body(): lax.all_to_all(blocks.reshape(plain.shape), ('x', 'z'), 0, 0, tiled=True)]
where the time goes in v4:
time: 80 us; the launch traced here: 79.6 us
  blocking collectives  37.2 us (47%)
  Pallas kernels  19.9 us (25%)
  starting transfers between devices  10.4 us (13%)
  waiting for transfers between devices  9.67 us (12%)
  other arithmetic  1.6 us (2%)
    pallas_call x7, Pallas kernels, call(): pl.pallas_call(kernel, out_shape=outs, in_specs=specs or [VMEM] * len(arg...  19.9 us
    all_to_all x2, blocking collectives, body(): ends = lax.all_to_all(ends, plane, 0, 0, tiled=True)  17.2 us
    all_to_all x1, blocking collectives, body(): b0 = lax.all_to_all(u0, plane, 0, 0, tiled=True)  11.3 us
    all_to_all x1, blocking collectives, body(): u = lax.all_to_all(states, plane, 0, 0, tiled=True)  8.62 us
    all_to_all x1, starting transfers between devices, body(): lax.all_to_all(blocks.reshape(plain.shape), ('x', 'z'), 0, 0, tiled=True)  5.81 us
    all_to_all x1, waiting for transfers between devices, body(): lax.all_to_all(blocks.reshape(plain.shape), ('x', 'z'), 0, 0, tiled=True)  5.44 us
    ppermute x2, starting transfers between devices, gather_from(): lax.ppermute(a, axis, [(i, (i + k) % n) for i in range(n)])  3.1 us
    ppermute x1, waiting for transfers between devices, body(): lax.ppermute(mine[k], 'x', [(i, (i + k) % inner) for i in range(inner)])  2.47 us
  transfers between devices with their start and end apart: 4, of which 3 were waited for; matrix products, arithmetic and copies ran while one was open for 1% of the time, Pallas kernels for 2%

profile of v4, /device:TPU:0, one launch (start us, length us, event | category | flops | bytes accessed | tf_op | source)
XLA Modules:
  0.0 79.6 jit_solution(10881192893405980506)
XLA Ops:
  0.7 2.2 %pack.1 = (f32[13,32,128]{2,1,0:T(8,128)}, f32[2,4,2,32,128]{4,3,2,1,0:T(8,128)}, f32[4,32,128]{2,1,0:T(8,128)}) custom-call(f32[4,32,128]{2,1,0:T(8,128)} %refs_0_.1, f32[4,32,128]{2,1,0:T(8,128)} %refs_1_.1, f32[4,32,128]{2,1,0:T(8,128)} %refs_2_.1, f32[4,32,128]{2,1,0:T(8,128)} %refs_3_.1, f32[1,4,32,128]{3,2,1,0:T(8,128)} %refs_4_.1, s32[8,128]{1,0:T(8,128)} %bitcast.22, ...), custom_call_target="tpu_custom_call" | custom-call | tf_op jit(solution)/shard_map/pack/pallas_call | solution.py:33
  2.9 0.0 copy-start
  2.9 3.0 %collective-permute-start = (f32[1,13,32,128]{3,2,1,0:T(8,128)}, f32[1,13,32,128]{3,2,1,0:T(8,128)S(1)}, u32[]{:S(2)}, u32[]{:S(2)}) collective-permute-start(f32[1,13,32,128]{3,2,1,0:T(8,128)} %bitcast.20), channel_id=1, source_target_pairs={{0,2},{2,0},{1,3},{3,1},{4,6},{6,4},{5,7},{7,5},{8,10},{10,8},{9,1... | collective-permute-start | bytes 638984 | tf_op jit(solution)/shard_map/ppermute | solution.py:431
  5.9 5.8 %all-to-all-start = ((f32[8,2,32,128]{3,2,1,0:T(8,128)}), f32[8,2,32,128]{3,2,1,0:T(8,128)S(1)}, u32[]{:S(2)}, u32[]{:S(2)}) async-start(f32[8,2,32,128]{3,2,1,0:T(8,128)} %bitcast.19), calls=%async_computation | async-start | bytes 524288 | tf_op jit(solution)/shard_map/all_to_all | solution.py:458
  11.7 0.0 collective-permute-done
  11.7 1.0 %pad_maximum_fusion.refs_0_ = f32[2,13,32,128]{3,2,1,0:T(8,128)S(1)} fusion(f32[1,13,32,128]{3,2,1,0:T(8,128)S(1)} %collective-permute-done, f32[1,13,32,128]{3,2,1,0:T(8,128)} %bitcast.21), kind=kLoop, calls=%fused_computation | loop fusion | flops 106496 | bytes 851968 | tf_op jit(solution)/shard_map/concatenate | solution.py:459
  12.7 0.1 collective-permute-start.1
  12.8 1.8 %collective-permute-done.1.refs_1_ = f32[2,13,32,128]{3,2,1,0:T(8,128)S(1)} collective-permute-done((f32[2,13,32,128]{3,2,1,0:T(8,128)S(1)}, f32[2,13,32,128]{3,2,1,0:T(8,128)S(1)}, u32[]{:S(2)}, u32[]{:S(2)}) %collective-permute-start.1) | collective-permute-done | bytes 426016 | tf_op jit(solution)/shard_map/ppermute | solution.py:431
  14.6 1.4 %prep.1 = (f32[4,8,2,32,128]{4,3,2,1,0:T(8,128)S(1)}, f32[4,32,128]{2,1,0:T(8,128)S(1)}, bf16[4,1024,256]{2,1,0:T(8,128)(2,1)S(1)}) custom-call(f32[2,13,32,128]{3,2,1,0:T(8,128)S(1)} %pad_maximum_fusion.refs_0_, f32[2,13,32,128]{3,2,1,0:T(8,128)S(1)} %collective-permute-done.1.refs_1_), custom_call_target="tpu_custom_call" | custom-call | tf_op jit(solution)/shard_map/prep/pallas_call | solution.py:33
  16.0 5.4 %all-to-all-done.refs_2_ = f32[8,2,32,128]{3,2,1,0:T(8,128)S(1)} async-done(((f32[8,2,32,128]{3,2,1,0:T(8,128)}), f32[8,2,32,128]{3,2,1,0:T(8,128)S(1)}, u32[]{:S(2)}, u32[]{:S(2)}) %all-to-all-start) | async-done | bytes 262176 | tf_op jit(solution)/shard_map/all_to_all | solution.py:458
  21.4 0.0 copy-done
  21.4 1.3 %chain0.1.refs_4_ = f32[8,2,2,32,128]{4,3,2,1,0:T(8,128)S(1)} custom-call(f32[4,32,128]{2,1,0:T(8,128)S(1)} %copy-done, f32[4,8,2,32,128]{4,3,2,1,0:T(8,128)S(1)} %get-tuple-element.23.refs_1_.fld_ref, f32[8,2,32,128]{3,2,1,0:T(8,128)S(1)} %all-to-all-done.refs_2_), custom_call_target="tpu_custom_call" | custom-call | tf_op jit(solution)/shard_map/chain0/pallas_call | solution.py:33
  22.7 11.3 %all_to_all.25.u_ref.s_ref = f32[8,2,2,32,128]{4,3,2,1,0:T(8,128)S(1)} all-to-all(f32[8,2,2,32,128]{4,3,2,1,0:T(8,128)S(1)} %chain0.1.refs_4_), channel_id=1, replica_groups=mesh['z'=4,'x'=2,'fo'=2,'fi'=2] {'x','fo','fi'}, dimensions={0} | all-to-all | bytes 1048576 | tf_op jit(solution)/shard_map/all_to_all | solution.py:476
  34.0 6.4 %fine.2 = f32[8,2,32,128]{3,2,1,0:T(8,128)S(1)} custom-call(f32[8,2,2,32,128]{4,3,2,1,0:T(8,128)S(1)} %all_to_all.25.u_ref.s_ref, f32[8,2,2,32,128]{4,3,2,1,0:T(8,128)S(1)} %all_to_all.25.u_ref.s_ref, f32[4,8,2,32,128]{4,3,2,1,0:T(8,128)S(1)} %get-tuple-element.23.refs_1_.fld_ref, f32[4,32,128]{2,1,0:T(8,128)S(1)} %get-tuple-element.25.ent_ref, ...), custom_call_target="tpu_custom_call" | custom-call | tf_op jit(solution)/shard_map/fine/pallas_call | solution.py:33
  40.5 8.6 %all_to_all.26.refs_3_ = f32[8,2,32,128]{3,2,1,0:T(8,128)S(1)} all-to-all(f32[8,2,32,128]{3,2,1,0:T(8,128)S(1)} %fine.2), channel_id=1, replica_groups=mesh['z'=4,'x'=2,'fo'=2,'fi'=2] {'x','fo','fi'}, dimensions={0} | all-to-all | bytes 524288 | tf_op jit(solution)/shard_map/all_to_all | solution.py:486
  49.1 1.1 %chain1.1 = (f32[8,2,32,128]{3,2,1,0:T(8,128)S(1)}, f32[8,2,32,128]{3,2,1,0:T(8,128)S(1)}) custom-call(f32[4,32,128]{2,1,0:T(8,128)S(1)} %copy-done, f32[4,8,2,32,128]{4,3,2,1,0:T(8,128)S(1)} %get-tuple-element.23.refs_1_.fld_ref, f32[8,2,32,128]{3,2,1,0:T(8,128)S(1)} %all-to-all-done.refs_2_, f32[8,2,32,128]{3,2,1,0:T(8,128)S(1)} %all_to_all.26.refs_3_, ...), custom_call_target="tpu_custom_call" | custom-call | tf_op jit(solution)/shard_map/chain1/pallas_call | solution.py:33
  50.2 8.6 %all_to_all.27.u_ref = f32[8,2,32,128]{3,2,1,0:T(8,128)S(1)} all-to-all(f32[8,2,32,128]{3,2,1,0:T(8,128)S(1)} %get-tuple-element.27), channel_id=1, replica_groups=mesh['z'=4,'x'=2,'fo'=2,'fi'=2] {'x','fo','fi'}, dimensions={0} | all-to-all | bytes 524288 | tf_op jit(solution)/shard_map/all_to_all | solution.py:489
  58.8 6.4 %fine.3 = f32[8,2,32,128]{3,2,1,0:T(8,128)S(1)} custom-call(f32[8,2,32,128]{3,2,1,0:T(8,128)S(1)} %all_to_all.27.u_ref, f32[8,2,2,32,128]{4,3,2,1,0:T(8,128)S(1)} %all_to_all.25.u_ref.s_ref, f32[4,8,2,32,128]{4,3,2,1,0:T(8,128)S(1)} %get-tuple-element.23.refs_1_.fld_ref, f32[4,32,128]{2,1,0:T(8,128)S(1)} %get-tuple-element.25.ent_ref, ...), custom_call_target="tpu_custom_call" | custom-call | tf_op jit(solution)/shard_map/fine/pallas_call | solution.py:33
  65.3 8.6 %all_to_all.28.refs_3_ = f32[8,2,32,128]{3,2,1,0:T(8,128)S(1)} all-to-all(f32[8,2,32,128]{3,2,1,0:T(8,128)S(1)} %fine.3), channel_id=1, replica_groups=mesh['z'=4,'x'=2,'fo'=2,'fi'=2] {'x','fo','fi'}, dimensions={0} | all-to-all | bytes 524288 | tf_op jit(solution)/shard_map/all_to_all | solution.py:486
  73.9 1.0 %chain2.1 = f32[2,2,32,128]{3,2,1,0:T(8,128)S(1)} custom-call(f32[4,32,128]{2,1,0:T(8,128)S(1)} %copy-done, f32[4,8,2,32,128]{4,3,2,1,0:T(8,128)S(1)} %get-tuple-element.23.refs_1_.fld_ref, f32[8,2,32,128]{3,2,1,0:T(8,128)S(1)} %all-to-all-done.refs_2_, f32[8,2,32,128]{3,2,1,0:T(8,128)S(1)} %all_to_all.28.refs_3_, ...), custom_call_target="tpu_custom_call" | custom-call | tf_op jit(solution)/shard_map/chain2/pallas_call | solution.py:33
  74.9 1.5 %collective-permute-start.2 = (f32[2,32,128]{2,1,0:T(8,128)S(1)}, f32[2,32,128]{2,1,0:T(8,128)S(1)}, u32[]{:S(2)}, u32[]{:S(2)}) collective-permute-start(f32[2,32,128]{2,1,0:T(8,128)S(1)} %slice_bitcast_fusion), channel_id=1, source_target_pairs={{0,4},{4,0},{1,5},{5,1},{2,6},{6,2},{3,7},{7,3},{8,12},{12,8},{9,1... | collective-permute-start | bytes 98312 | tf_op jit(solution)/shard_map/ppermute | solution.py:499
  76.4 2.5 %collective-permute-done.2 = f32[2,32,128]{2,1,0:T(8,128)S(1)} collective-permute-done((f32[2,32,128]{2,1,0:T(8,128)S(1)}, f32[2,32,128]{2,1,0:T(8,128)S(1)}, u32[]{:S(2)}, u32[]{:S(2)}) %collective-permute-start.2) | collective-permute-done | bytes 32800 | tf_op jit(solution)/shard_map/ppermute | solution.py:499
  78.9 0.6 pad_maximum_fusion.1
  (2 shorter events, 0.0 us)
Async XLA Ops:
  2.9 18.5 %copy-start = (f32[4,32,128]{2,1,0:T(8,128)S(1)}, f32[4,32,128]{2,1,0:T(8,128)}, u32[]{:S(2)}) copy-start(f32[4,32,128]{2,1,0:T(8,128)} %get-tuple-element.17.refs_0_) | copy-start | bytes 196612
  2.9 8.8 %collective-permute-start = (f32[1,13,32,128]{3,2,1,0:T(8,128)}, f32[1,13,32,128]{3,2,1,0:T(8,128)S(1)}, u32[]{:S(2)}, u32[]{:S(2)}) collective-permute-start(f32[1,13,32,128]{3,2,1,0:T(8,128)} %bitcast.20), channel_id=1, source_target_pairs={{0,2},{2,0},{1,3},{3,1},{4,6},{6,4},{5,7},{7,5},{8,10},{10,8},{9,1... | collective-permute-start | bytes 638984 | tf_op jit(solution)/shard_map/ppermute | solution.py:431
  5.9 15.5 %all-to-all-start = ((f32[8,2,32,128]{3,2,1,0:T(8,128)}), f32[8,2,32,128]{3,2,1,0:T(8,128)S(1)}, u32[]{:S(2)}, u32[]{:S(2)}) async-start(f32[8,2,32,128]{3,2,1,0:T(8,128)} %bitcast.19), calls=%async_computation | async-start | bytes 524288 | tf_op jit(solution)/shard_map/all_to_all | solution.py:458
  12.7 1.8 %collective-permute-start.1 = (f32[2,13,32,128]{3,2,1,0:T(8,128)S(1)}, f32[2,13,32,128]{3,2,1,0:T(8,128)S(1)}, u32[]{:S(2)}, u32[]{:S(2)}) collective-permute-start(f32[2,13,32,128]{3,2,1,0:T(8,128)S(1)} %pad_maximum_fusion.refs_0_), channel_id=1, source_target_pairs={{0,1},{1,0},{2,3},{3,2},{4,5},{5,4},{6,7},{7,6},{8,9},{9,8},{10,11... | collective-permute-start | bytes 1277960 | tf_op jit(solution)/shard_map/ppermute | solution.py:431
  74.9 4.0 %collective-permute-start.2 = (f32[2,32,128]{2,1,0:T(8,128)S(1)}, f32[2,32,128]{2,1,0:T(8,128)S(1)}, u32[]{:S(2)}, u32[]{:S(2)}) collective-permute-start(f32[2,32,128]{2,1,0:T(8,128)S(1)} %slice_bitcast_fusion), channel_id=1, source_target_pairs={{0,4},{4,0},{1,5},{5,1},{2,6},{6,2},{3,7},{7,3},{8,12},{12,8},{9,1... | collective-permute-start | bytes 98312 | tf_op jit(solution)/shard_map/ppermute | solution.py:499

commit v5 on v4

--- a/solution.py
+++ b/solution.py
@@ -307,21 +307,25 @@
         for e in range(export_rows):
             at = jnp.broadcast_to(cell[e : e + 1, :], (SUBS, LANES))
             row, col = at // LANES - iota, at % LANES
-            found = [jnp.zeros((SUBS, LANES), F32) for _ in range(2)]
+            found = [jnp.zeros((SUBS, LANES), F32) for _ in range(4)]
             for t in range(rows // SUBS):
                 slot, r = t * SUBS // frac_rows, t * SUBS % frac_rows
                 got = pick_lanes(o_ref[slot // own * parts + d, slot % own, r : r + SUBS, :], col)
-                found[t % 2] = jnp.where(row == t * SUBS, got, found[t % 2])
-            exported.append(jnp.sum(found[0] + found[1], axis=0, keepdims=True))
+                found[t % 4] = jnp.where(row == t * SUBS, got, found[t % 4])
+            every = (found[0] + found[1]) + (found[2] + found[3])
+            for turn in (4, 2, 1):
+                every = every + pltpu.roll(every, turn, axis=0)
+            exported.append(every)
     out = []
     for d in range(parts):
         slot = layout.entries(ent_ref, d, 1).astype(jnp.int32)
         row, col = slot // LANES, slot % LANES
-        x = jnp.zeros(slot.shape, F32)
+        x = [jnp.zeros(slot.shape, F32) for _ in range(2)]
         for t in range(parts * export_rows):
             if t // export_rows != d:
-                got = pick_lanes(jnp.broadcast_to(exported[t], slot.shape), col)
-                x = jnp.where(row == t, got, x)
+                got = pick_lanes(jnp.concatenate([exported[t]] * (slot.shape[0] // SUBS), axis=0), col)
+                x[t % 2] = jnp.where(row == t, got, x[t % 2])
+        x = x[0] + x[1]
         out.append(layout.entries(ent_ref, d, 2) * x)
     return out
 

time: 80 us -> 79.9 us (level)
  no operation moved by 1% of the time
where the time goes in v5:
time: 79.9 us; the launch traced here: 79.5 us
  blocking collectives  37.2 us (47%)
  Pallas kernels  19.9 us (25%)
  starting transfers between devices  10.4 us (13%)
  waiting for transfers between devices  9.67 us (12%)
  other arithmetic  1.6 us (2%)
    pallas_call x7, Pallas kernels, call(): pl.pallas_call(kernel, out_shape=outs, in_specs=specs or [VMEM] * len(arg...  19.9 us
    all_to_all x2, blocking collectives, body(): ends = lax.all_to_all(ends, plane, 0, 0, tiled=True)  17.2 us
    all_to_all x1, blocking collectives, body(): b0 = lax.all_to_all(u0, plane, 0, 0, tiled=True)  11.3 us
    all_to_all x1, blocking collectives, body(): u = lax.all_to_all(states, plane, 0, 0, tiled=True)  8.62 us
    all_to_all x1, starting transfers between devices, body(): lax.all_to_all(blocks.reshape(plain.shape), ('x', 'z'), 0, 0, tiled=True)  5.81 us
    all_to_all x1, waiting for transfers between devices, body(): lax.all_to_all(blocks.reshape(plain.shape), ('x', 'z'), 0, 0, tiled=True)  5.44 us
    ppermute x2, starting transfers between devices, gather_from(): lax.ppermute(a, axis, [(i, (i + k) % n) for i in range(n)])  3.1 us
    ppermute x1, waiting for transfers between devices, body(): lax.ppermute(mine[k], 'x', [(i, (i + k) % inner) for i in range(inner)])  2.47 us
  transfers between devices with their start and end apart: 4, of which 3 were waited for; matrix products, arithmetic and copies ran while one was open for 1% of the time, Pallas kernels for 2%

profile of v5, /device:TPU:0, one launch (start us, length us, event | category | flops | bytes accessed | tf_op | source)
XLA Modules:
  0.0 79.5 jit_solution(8419368667117497254)
XLA Ops:
  0.7 2.2 %pack.1 = (f32[13,32,128]{2,1,0:T(8,128)}, f32[2,4,2,32,128]{4,3,2,1,0:T(8,128)}, f32[4,32,128]{2,1,0:T(8,128)}) custom-call(f32[4,32,128]{2,1,0:T(8,128)} %refs_0_.1, f32[4,32,128]{2,1,0:T(8,128)} %refs_1_.1, f32[4,32,128]{2,1,0:T(8,128)} %refs_2_.1, f32[4,32,128]{2,1,0:T(8,128)} %refs_3_.1, f32[1,4,32,128]{3,2,1,0:T(8,128)} %refs_4_.1, s32[8,128]{1,0:T(8,128)} %bitcast.22, ...), custom_call_target="tpu_custom_call" | custom-call | tf_op jit(solution)/shard_map/pack/pallas_call | solution.py:33
  2.9 0.0 copy-start
  2.9 3.0 %collective-permute-start = (f32[1,13,32,128]{3,2,1,0:T(8,128)}, f32[1,13,32,128]{3,2,1,0:T(8,128)S(1)}, u32[]{:S(2)}, u32[]{:S(2)}) collective-permute-start(f32[1,13,32,128]{3,2,1,0:T(8,128)} %bitcast.20), channel_id=1, source_target_pairs={{0,2},{2,0},{1,3},{3,1},{4,6},{6,4},{5,7},{7,5},{8,10},{10,8},{9,1... | collective-permute-start | bytes 638984 | tf_op jit(solution)/shard_map/ppermute | solution.py:435
  5.9 5.8 %all-to-all-start = ((f32[8,2,32,128]{3,2,1,0:T(8,128)}), f32[8,2,32,128]{3,2,1,0:T(8,128)S(1)}, u32[]{:S(2)}, u32[]{:S(2)}) async-start(f32[8,2,32,128]{3,2,1,0:T(8,128)} %bitcast.19), calls=%async_computation | async-start | bytes 524288 | tf_op jit(solution)/shard_map/all_to_all | solution.py:462
  11.7 0.0 collective-permute-done
  11.7 1.0 %pad_maximum_fusion.refs_0_ = f32[2,13,32,128]{3,2,1,0:T(8,128)S(1)} fusion(f32[1,13,32,128]{3,2,1,0:T(8,128)S(1)} %collective-permute-done, f32[1,13,32,128]{3,2,1,0:T(8,128)} %bitcast.21), kind=kLoop, calls=%fused_computation | loop fusion | flops 106496 | bytes 851968 | tf_op jit(solution)/shard_map/concatenate | solution.py:463
  12.7 0.1 collective-permute-start.1
  12.8 1.8 %collective-permute-done.1.refs_1_ = f32[2,13,32,128]{3,2,1,0:T(8,128)S(1)} collective-permute-done((f32[2,13,32,128]{3,2,1,0:T(8,128)S(1)}, f32[2,13,32,128]{3,2,1,0:T(8,128)S(1)}, u32[]{:S(2)}, u32[]{:S(2)}) %collective-permute-start.1) | collective-permute-done | bytes 426016 | tf_op jit(solution)/shard_map/ppermute | solution.py:435
  14.6 1.4 %prep.1 = (f32[4,8,2,32,128]{4,3,2,1,0:T(8,128)S(1)}, f32[4,32,128]{2,1,0:T(8,128)S(1)}, bf16[4,1024,256]{2,1,0:T(8,128)(2,1)S(1)}) custom-call(f32[2,13,32,128]{3,2,1,0:T(8,128)S(1)} %pad_maximum_fusion.refs_0_, f32[2,13,32,128]{3,2,1,0:T(8,128)S(1)} %collective-permute-done.1.refs_1_), custom_call_target="tpu_custom_call" | custom-call | tf_op jit(solution)/shard_map/prep/pallas_call | solution.py:33
  16.0 5.4 %all-to-all-done.refs_2_ = f32[8,2,32,128]{3,2,1,0:T(8,128)S(1)} async-done(((f32[8,2,32,128]{3,2,1,0:T(8,128)}), f32[8,2,32,128]{3,2,1,0:T(8,128)S(1)}, u32[]{:S(2)}, u32[]{:S(2)}) %all-to-all-start) | async-done | bytes 262176 | tf_op jit(solution)/shard_map/all_to_all | solution.py:462
  21.4 0.0 copy-done
  21.4 1.3 %chain0.1.refs_4_ = f32[8,2,2,32,128]{4,3,2,1,0:T(8,128)S(1)} custom-call(f32[4,32,128]{2,1,0:T(8,128)S(1)} %copy-done, f32[4,8,2,32,128]{4,3,2,1,0:T(8,128)S(1)} %get-tuple-element.23.refs_1_.fld_ref, f32[8,2,32,128]{3,2,1,0:T(8,128)S(1)} %all-to-all-done.refs_2_), custom_call_target="tpu_custom_call" | custom-call | tf_op jit(solution)/shard_map/chain0/pallas_call | solution.py:33
  22.7 11.3 %all_to_all.25.u_ref.s_ref = f32[8,2,2,32,128]{4,3,2,1,0:T(8,128)S(1)} all-to-all(f32[8,2,2,32,128]{4,3,2,1,0:T(8,128)S(1)} %chain0.1.refs_4_), channel_id=1, replica_groups=mesh['z'=4,'x'=2,'fo'=2,'fi'=2] {'x','fo','fi'}, dimensions={0} | all-to-all | bytes 1048576 | tf_op jit(solution)/shard_map/all_to_all | solution.py:480
  34.0 6.4 %fine.2 = f32[8,2,32,128]{3,2,1,0:T(8,128)S(1)} custom-call(f32[8,2,2,32,128]{4,3,2,1,0:T(8,128)S(1)} %all_to_all.25.u_ref.s_ref, f32[8,2,2,32,128]{4,3,2,1,0:T(8,128)S(1)} %all_to_all.25.u_ref.s_ref, f32[4,8,2,32,128]{4,3,2,1,0:T(8,128)S(1)} %get-tuple-element.23.refs_1_.fld_ref, f32[4,32,128]{2,1,0:T(8,128)S(1)} %get-tuple-element.25.ent_ref, ...), custom_call_target="tpu_custom_call" | custom-call | tf_op jit(solution)/shard_map/fine/pallas_call | solution.py:33
  40.4 8.6 %all_to_all.26.refs_3_ = f32[8,2,32,128]{3,2,1,0:T(8,128)S(1)} all-to-all(f32[8,2,32,128]{3,2,1,0:T(8,128)S(1)} %fine.2), channel_id=1, replica_groups=mesh['z'=4,'x'=2,'fo'=2,'fi'=2] {'x','fo','fi'}, dimensions={0} | all-to-all | bytes 524288 | tf_op jit(solution)/shard_map/all_to_all | solution.py:490
  49.1 1.1 %chain1.1 = (f32[8,2,32,128]{3,2,1,0:T(8,128)S(1)}, f32[8,2,32,128]{3,2,1,0:T(8,128)S(1)}) custom-call(f32[4,32,128]{2,1,0:T(8,128)S(1)} %copy-done, f32[4,8,2,32,128]{4,3,2,1,0:T(8,128)S(1)} %get-tuple-element.23.refs_1_.fld_ref, f32[8,2,32,128]{3,2,1,0:T(8,128)S(1)} %all-to-all-done.refs_2_, f32[8,2,32,128]{3,2,1,0:T(8,128)S(1)} %all_to_all.26.refs_3_, ...), custom_call_target="tpu_custom_call" | custom-call | tf_op jit(solution)/shard_map/chain1/pallas_call | solution.py:33
  50.2 8.6 %all_to_all.27.u_ref = f32[8,2,32,128]{3,2,1,0:T(8,128)S(1)} all-to-all(f32[8,2,32,128]{3,2,1,0:T(8,128)S(1)} %get-tuple-element.27), channel_id=1, replica_groups=mesh['z'=4,'x'=2,'fo'=2,'fi'=2] {'x','fo','fi'}, dimensions={0} | all-to-all | bytes 524288 | tf_op jit(solution)/shard_map/all_to_all | solution.py:493
  58.8 6.4 %fine.3 = f32[8,2,32,128]{3,2,1,0:T(8,128)S(1)} custom-call(f32[8,2,32,128]{3,2,1,0:T(8,128)S(1)} %all_to_all.27.u_ref, f32[8,2,2,32,128]{4,3,2,1,0:T(8,128)S(1)} %all_to_all.25.u_ref.s_ref, f32[4,8,2,32,128]{4,3,2,1,0:T(8,128)S(1)} %get-tuple-element.23.refs_1_.fld_ref, f32[4,32,128]{2,1,0:T(8,128)S(1)} %get-tuple-element.25.ent_ref, ...), custom_call_target="tpu_custom_call" | custom-call | tf_op jit(solution)/shard_map/fine/pallas_call | solution.py:33
  65.2 8.6 %all_to_all.28.refs_3_ = f32[8,2,32,128]{3,2,1,0:T(8,128)S(1)} all-to-all(f32[8,2,32,128]{3,2,1,0:T(8,128)S(1)} %fine.3), channel_id=1, replica_groups=mesh['z'=4,'x'=2,'fo'=2,'fi'=2] {'x','fo','fi'}, dimensions={0} | all-to-all | bytes 524288 | tf_op jit(solution)/shard_map/all_to_all | solution.py:490
  73.8 1.0 %chain2.1 = f32[2,2,32,128]{3,2,1,0:T(8,128)S(1)} custom-call(f32[4,32,128]{2,1,0:T(8,128)S(1)} %copy-done, f32[4,8,2,32,128]{4,3,2,1,0:T(8,128)S(1)} %get-tuple-element.23.refs_1_.fld_ref, f32[8,2,32,128]{3,2,1,0:T(8,128)S(1)} %all-to-all-done.refs_2_, f32[8,2,32,128]{3,2,1,0:T(8,128)S(1)} %all_to_all.28.refs_3_, ...), custom_call_target="tpu_custom_call" | custom-call | tf_op jit(solution)/shard_map/chain2/pallas_call | solution.py:33
  74.9 1.5 %collective-permute-start.2 = (f32[2,32,128]{2,1,0:T(8,128)S(1)}, f32[2,32,128]{2,1,0:T(8,128)S(1)}, u32[]{:S(2)}, u32[]{:S(2)}) collective-permute-start(f32[2,32,128]{2,1,0:T(8,128)S(1)} %slice_bitcast_fusion), channel_id=1, source_target_pairs={{0,4},{4,0},{1,5},{5,1},{2,6},{6,2},{3,7},{7,3},{8,12},{12,8},{9,1... | collective-permute-start | bytes 98312 | tf_op jit(solution)/shard_map/ppermute | solution.py:503
  76.4 2.5 %collective-permute-done.2 = f32[2,32,128]{2,1,0:T(8,128)S(1)} collective-permute-done((f32[2,32,128]{2,1,0:T(8,128)S(1)}, f32[2,32,128]{2,1,0:T(8,128)S(1)}, u32[]{:S(2)}, u32[]{:S(2)}) %collective-permute-start.2) | collective-permute-done | bytes 32800 | tf_op jit(solution)/shard_map/ppermute | solution.py:503
  78.9 0.6 pad_maximum_fusion.1
  (2 shorter events, 0.0 us)
Async XLA Ops:
  2.9 18.5 %copy-start = (f32[4,32,128]{2,1,0:T(8,128)S(1)}, f32[4,32,128]{2,1,0:T(8,128)}, u32[]{:S(2)}) copy-start(f32[4,32,128]{2,1,0:T(8,128)} %get-tuple-element.17.refs_0_) | copy-start | bytes 196612
  2.9 8.8 %collective-permute-start = (f32[1,13,32,128]{3,2,1,0:T(8,128)}, f32[1,13,32,128]{3,2,1,0:T(8,128)S(1)}, u32[]{:S(2)}, u32[]{:S(2)}) collective-permute-start(f32[1,13,32,128]{3,2,1,0:T(8,128)} %bitcast.20), channel_id=1, source_target_pairs={{0,2},{2,0},{1,3},{3,1},{4,6},{6,4},{5,7},{7,5},{8,10},{10,8},{9,1... | collective-permute-start | bytes 638984 | tf_op jit(solution)/shard_map/ppermute | solution.py:435
  5.9 15.5 %all-to-all-start = ((f32[8,2,32,128]{3,2,1,0:T(8,128)}), f32[8,2,32,128]{3,2,1,0:T(8,128)S(1)}, u32[]{:S(2)}, u32[]{:S(2)}) async-start(f32[8,2,32,128]{3,2,1,0:T(8,128)} %bitcast.19), calls=%async_computation | async-start | bytes 524288 | tf_op jit(solution)/shard_map/all_to_all | solution.py:462
  12.7 1.8 %collective-permute-start.1 = (f32[2,13,32,128]{3,2,1,0:T(8,128)S(1)}, f32[2,13,32,128]{3,2,1,0:T(8,128)S(1)}, u32[]{:S(2)}, u32[]{:S(2)}) collective-permute-start(f32[2,13,32,128]{3,2,1,0:T(8,128)S(1)} %pad_maximum_fusion.refs_0_), channel_id=1, source_target_pairs={{0,1},{1,0},{2,3},{3,2},{4,5},{5,4},{6,7},{7,6},{8,9},{9,8},{10,11... | collective-permute-start | bytes 1277960 | tf_op jit(solution)/shard_map/ppermute | solution.py:435
  74.9 4.0 %collective-permute-start.2 = (f32[2,32,128]{2,1,0:T(8,128)S(1)}, f32[2,32,128]{2,1,0:T(8,128)S(1)}, u32[]{:S(2)}, u32[]{:S(2)}) collective-permute-start(f32[2,32,128]{2,1,0:T(8,128)S(1)} %slice_bitcast_fusion), channel_id=1, source_target_pairs={{0,4},{4,0},{1,5},{5,1},{2,6},{6,2},{3,7},{7,3},{8,12},{12,8},{9,1... | collective-permute-start | bytes 98312 | tf_op jit(solution)/shard_map/ppermute | solution.py:503

commit v6 on v4

--- a/solution.py
+++ b/solution.py
@@ -498,7 +498,10 @@
     got = [mine[0]] + [
         lax.ppermute(mine[k], "x", [(i, (i + k) % inner) for i in range(inner)]) for k in range(1, inner)
     ]
-    return jnp.stack([lax.select_n((x - i) % inner, *got) if inner > 2 else jnp.where(x == i, got[0], got[-1]) for i in range(inner)]).reshape(1, held, frac_rows, LANES)
+    out = jnp.zeros((held, frac_rows, LANES), F32)
+    for k in range(inner):
+        out = lax.dynamic_update_slice_in_dim(out, got[k], (x - k) % inner * own, 0)
+    return out[None]
 
 
 def solution(mesh):

time: 80 us -> 83.2 us (1.040)
  blocking collectives: 37.2 us -> 28.5 us
  waiting for transfers between devices: 9.67 us -> 15.6 us
  starting transfers between devices: 10.4 us -> 13.8 us
  local copies, waits for them, and re-layouts: 0.01 us -> 2.98 us
    all_to_all x2 -> x1, blocking collectives: 17.2 us -> 8.62 us  [body(): ends = lax.all_to_all(ends, plane, 0, 0, tiled=True)]
    all_to_all x0 -> x1, waiting for transfers between devices: none -> 5.96 us  [body(): ends = lax.all_to_all(ends, plane, 0, 0, tiled=True)]
    all_to_all x0 -> x1, starting transfers between devices: none -> 3.41 us  [body(): ends = lax.all_to_all(ends, plane, 0, 0, tiled=True)]
    unnamed x2 -> x10, local copies, waits for them, and re-layouts: 0.01 us -> 2.35 us
  transfers between devices with their start and end apart: 4 -> 5, of which waited for: 3 -> 4; matrix products, arithmetic and copies ran while one was open for 1% -> 1% of each run, Pallas kernels for 2% -> 2%
where the time goes in v6:
time: 83.2 us; the launch traced here: 82.7 us
  blocking collectives  28.5 us (34%)
  Pallas kernels  19.9 us (24%)
  waiting for transfers between devices  15.6 us (19%)
  starting transfers between devices  13.8 us (17%)
  local copies, waits for them, and re-layouts  2.98 us (4%)
  other arithmetic  0.96 us (1%)
    pallas_call x7, Pallas kernels, call(): pl.pallas_call(kernel, out_shape=outs, in_specs=specs or [VMEM] * len(arg...  19.9 us
    all_to_all x1, blocking collectives, body(): b0 = lax.all_to_all(u0, plane, 0, 0, tiled=True)  11.3 us
    all_to_all x1, blocking collectives, body(): ends = lax.all_to_all(ends, plane, 0, 0, tiled=True)  8.62 us
    all_to_all x1, blocking collectives, body(): u = lax.all_to_all(states, plane, 0, 0, tiled=True)  8.61 us
    all_to_all x1, waiting for transfers between devices, body(): ends = lax.all_to_all(ends, plane, 0, 0, tiled=True)  5.96 us
    all_to_all x1, starting transfers between devices, body(): lax.all_to_all(blocks.reshape(plain.shape), ('x', 'z'), 0, 0, tiled=True)  5.81 us
    all_to_all x1, waiting for transfers between devices, body(): lax.all_to_all(blocks.reshape(plain.shape), ('x', 'z'), 0, 0, tiled=True)  5.44 us
    all_to_all x1, starting transfers between devices, body(): ends = lax.all_to_all(ends, plane, 0, 0, tiled=True)  3.41 us
  transfers between devices with their start and end apart: 5, of which 4 were waited for; matrix products, arithmetic and copies ran while one was open for 1% of the time, Pallas kernels for 2%

profile of v6, /device:TPU:0, one launch (start us, length us, event | category | flops | bytes accessed | tf_op | source)
XLA Modules:
  0.0 82.7 jit_solution(1527226657321944704)
XLA Ops:
  0.7 2.2 %pack.1 = (f32[13,32,128]{2,1,0:T(8,128)}, f32[2,4,2,32,128]{4,3,2,1,0:T(8,128)}, f32[4,32,128]{2,1,0:T(8,128)}) custom-call(f32[4,32,128]{2,1,0:T(8,128)} %refs_0_.1, f32[4,32,128]{2,1,0:T(8,128)} %refs_1_.1, f32[4,32,128]{2,1,0:T(8,128)} %refs_2_.1, f32[4,32,128]{2,1,0:T(8,128)} %refs_3_.1, f32[1,4,32,128]{3,2,1,0:T(8,128)} %refs_4_.1, s32[8,128]{1,0:T(8,128)} %bitcast.13, ...), custom_call_target="tpu_custom_call" | custom-call | tf_op jit(solution)/shard_map/pack/pallas_call | solution.py:33
  2.9 0.0 copy-start.1
  2.9 3.0 %collective-permute-start = (f32[1,13,32,128]{3,2,1,0:T(8,128)}, f32[1,13,32,128]{3,2,1,0:T(8,128)S(1)}, u32[]{:S(2)}, u32[]{:S(2)}) collective-permute-start(f32[1,13,32,128]{3,2,1,0:T(8,128)} %bitcast.11), channel_id=1, source_target_pairs={{0,2},{2,0},{1,3},{3,1},{4,6},{6,4},{5,7},{7,5},{8,10},{10,8},{9,1... | collective-permute-start | bytes 638984 | tf_op jit(solution)/shard_map/ppermute | solution.py:431
  5.9 5.8 %all-to-all-start = ((f32[8,2,32,128]{3,2,1,0:T(8,128)}), f32[8,2,32,128]{3,2,1,0:T(8,128)S(1)}, u32[]{:S(2)}, u32[]{:S(2)}) async-start(f32[8,2,32,128]{3,2,1,0:T(8,128)} %bitcast.10), calls=%async_computation | async-start | bytes 524288 | tf_op jit(solution)/shard_map/all_to_all | solution.py:458
  11.7 0.0 collective-permute-done
  11.7 1.0 %pad_maximum_fusion.refs_0_ = f32[2,13,32,128]{3,2,1,0:T(8,128)S(1)} fusion(f32[1,13,32,128]{3,2,1,0:T(8,128)S(1)} %collective-permute-done, f32[1,13,32,128]{3,2,1,0:T(8,128)} %bitcast.12), kind=kLoop, calls=%fused_computation | loop fusion | flops 106496 | bytes 851968 | tf_op jit(solution)/shard_map/concatenate | solution.py:459
  12.7 0.1 collective-permute-start.1
  12.8 1.8 %collective-permute-done.1.refs_1_ = f32[2,13,32,128]{3,2,1,0:T(8,128)S(1)} collective-permute-done((f32[2,13,32,128]{3,2,1,0:T(8,128)S(1)}, f32[2,13,32,128]{3,2,1,0:T(8,128)S(1)}, u32[]{:S(2)}, u32[]{:S(2)}) %collective-permute-start.1) | collective-permute-done | bytes 426016 | tf_op jit(solution)/shard_map/ppermute | solution.py:431
  14.6 1.4 %prep.1 = (f32[4,8,2,32,128]{4,3,2,1,0:T(8,128)S(1)}, f32[4,32,128]{2,1,0:T(8,128)S(1)}, bf16[4,1024,256]{2,1,0:T(8,128)(2,1)S(1)}) custom-call(f32[2,13,32,128]{3,2,1,0:T(8,128)S(1)} %pad_maximum_fusion.refs_0_, f32[2,13,32,128]{3,2,1,0:T(8,128)S(1)} %collective-permute-done.1.refs_1_), custom_call_target="tpu_custom_call" | custom-call | tf_op jit(solution)/shard_map/prep/pallas_call | solution.py:33
  16.0 5.4 %all-to-all-done.refs_2_ = f32[8,2,32,128]{3,2,1,0:T(8,128)S(1)} async-done(((f32[8,2,32,128]{3,2,1,0:T(8,128)}), f32[8,2,32,128]{3,2,1,0:T(8,128)S(1)}, u32[]{:S(2)}, u32[]{:S(2)}) %all-to-all-start) | async-done | bytes 262176 | tf_op jit(solution)/shard_map/all_to_all | solution.py:458
  21.4 0.0 copy-done.1
  21.4 1.3 %chain0.1.refs_4_ = f32[8,2,2,32,128]{4,3,2,1,0:T(8,128)S(1)} custom-call(f32[4,32,128]{2,1,0:T(8,128)S(1)} %copy-done.1, f32[4,8,2,32,128]{4,3,2,1,0:T(8,128)S(1)} %get-tuple-element.23.refs_1_.fld_ref, f32[8,2,32,128]{3,2,1,0:T(8,128)S(1)} %all-to-all-done.refs_2_), custom_call_target="tpu_custom_call" | custom-call | tf_op jit(solution)/shard_map/chain0/pallas_call | solution.py:33
  22.7 11.3 %all_to_all.25.u_ref.s_ref = f32[8,2,2,32,128]{4,3,2,1,0:T(8,128)S(1)} all-to-all(f32[8,2,2,32,128]{4,3,2,1,0:T(8,128)S(1)} %chain0.1.refs_4_), channel_id=1, replica_groups=mesh['z'=4,'x'=2,'fo'=2,'fi'=2] {'x','fo','fi'}, dimensions={0} | all-to-all | bytes 1048576 | tf_op jit(solution)/shard_map/all_to_all | solution.py:476
  34.0 6.4 %fine.2 = f32[8,2,32,128]{3,2,1,0:T(8,128)S(1)} custom-call(f32[8,2,2,32,128]{4,3,2,1,0:T(8,128)S(1)} %all_to_all.25.u_ref.s_ref, f32[8,2,2,32,128]{4,3,2,1,0:T(8,128)S(1)} %all_to_all.25.u_ref.s_ref, f32[4,8,2,32,128]{4,3,2,1,0:T(8,128)S(1)} %get-tuple-element.23.refs_1_.fld_ref, f32[4,32,128]{2,1,0:T(8,128)S(1)} %get-tuple-element.25.ent_ref, ...), custom_call_target="tpu_custom_call" | custom-call | tf_op jit(solution)/shard_map/fine/pallas_call | solution.py:33
  40.5 8.6 %all_to_all.26.refs_3_ = f32[8,2,32,128]{3,2,1,0:T(8,128)S(1)} all-to-all(f32[8,2,32,128]{3,2,1,0:T(8,128)S(1)} %fine.2), channel_id=1, replica_groups=mesh['z'=4,'x'=2,'fo'=2,'fi'=2] {'x','fo','fi'}, dimensions={0} | all-to-all | bytes 524288 | tf_op jit(solution)/shard_map/all_to_all | solution.py:486
  49.1 1.1 %chain1.1 = (f32[8,2,32,128]{3,2,1,0:T(8,128)S(1)}, f32[8,2,32,128]{3,2,1,0:T(8,128)S(1)}) custom-call(f32[4,32,128]{2,1,0:T(8,128)S(1)} %copy-done.1, f32[4,8,2,32,128]{4,3,2,1,0:T(8,128)S(1)} %get-tuple-element.23.refs_1_.fld_ref, f32[8,2,32,128]{3,2,1,0:T(8,128)S(1)} %all-to-all-done.refs_2_, f32[8,2,32,128]{3,2,1,0:T(8,128)S(1)} %all_to_all.26.refs_3_, ...), custom_call_target="tpu_custom_call" | custom-call | tf_op jit(solution)/shard_map/chain1/pallas_call | solution.py:33
  50.2 0.0 copy-start.2
  50.2 0.7 copy-done.2
  50.9 8.6 %all_to_all.27.u_ref = f32[8,2,32,128]{3,2,1,0:T(8,128)S(1)} all-to-all(f32[8,2,32,128]{3,2,1,0:T(8,128)S(1)} %get-tuple-element.27), channel_id=1, replica_groups=mesh['z'=4,'x'=2,'fo'=2,'fi'=2] {'x','fo','fi'}, dimensions={0} | all-to-all | bytes 524288 | tf_op jit(solution)/shard_map/all_to_all | solution.py:489
  59.5 6.4 %fine.3 = f32[8,2,32,128]{3,2,1,0:T(8,128)S(1)} custom-call(f32[8,2,32,128]{3,2,1,0:T(8,128)S(1)} %all_to_all.27.u_ref, f32[8,2,2,32,128]{4,3,2,1,0:T(8,128)S(1)} %all_to_all.25.u_ref.s_ref, f32[4,8,2,32,128]{4,3,2,1,0:T(8,128)S(1)} %get-tuple-element.23.refs_1_.fld_ref, f32[4,32,128]{2,1,0:T(8,128)S(1)} %get-tuple-element.25.ent_ref, ...), custom_call_target="tpu_custom_call" | custom-call | tf_op jit(solution)/shard_map/fine/pallas_call | solution.py:33
  65.9 0.0 copy-start
  65.9 0.7 copy-done
  66.6 3.4 %all-to-all-start.4 = ((f32[8,2,32,128]{3,2,1,0:T(8,128)}), f32[8,2,32,128]{3,2,1,0:T(8,128)S(1)}, u32[]{:S(2)}, u32[]{:S(2)}) async-start(f32[8,2,32,128]{3,2,1,0:T(8,128)} %copy-done), calls=%async_computation.4 | async-start | bytes 524288 | tf_op jit(solution)/shard_map/all_to_all | solution.py:486
  70.1 6.0 %all-to-all-done.4.refs_3_ = f32[8,2,32,128]{3,2,1,0:T(8,128)S(1)} async-done(((f32[8,2,32,128]{3,2,1,0:T(8,128)}), f32[8,2,32,128]{3,2,1,0:T(8,128)S(1)}, u32[]{:S(2)}, u32[]{:S(2)}) %all-to-all-start.4) | async-done | bytes 262176 | tf_op jit(solution)/shard_map/all_to_all | solution.py:486
  76.0 0.0 copy-start.3
  76.0 0.9 %copy-done.3 = f32[8,2,32,128]{3,2,1,0:T(8,128)S(1)} copy-done((f32[8,2,32,128]{3,2,1,0:T(8,128)S(1)}, f32[8,2,32,128]{3,2,1,0:T(8,128)}, u32[]{:S(2)}) %copy-start.3) | copy-done | bytes 262168
  77.0 1.0 %chain2.1 = f32[2,2,32,128]{3,2,1,0:T(8,128)S(1)} custom-call(f32[4,32,128]{2,1,0:T(8,128)S(1)} %copy-done.1, f32[4,8,2,32,128]{4,3,2,1,0:T(8,128)S(1)} %get-tuple-element.23.refs_1_.fld_ref, f32[8,2,32,128]{3,2,1,0:T(8,128)S(1)} %all-to-all-done.refs_2_, f32[8,2,32,128]{3,2,1,0:T(8,128)S(1)} %all-to-all-done.4.refs_3_, f32[8,2,32,128]{3,2,1,0:T(8,128)S(1)} %copy-done.3), custom_call_target="tpu_custom_call" | custom-call | tf_op jit(solution)/shard_map/chain2/pallas_call | solution.py:33
  78.1 0.0 copy-start.4
  78.1 1.5 %collective-permute-start.2 = (f32[2,32,128]{2,1,0:T(8,128)S(1)}, f32[2,32,128]{2,1,0:T(8,128)S(1)}, u32[]{:S(2)}, u32[]{:S(2)}) collective-permute-start(f32[2,32,128]{2,1,0:T(8,128)S(1)} %get-tuple-element.29), channel_id=1, source_target_pairs={{0,4},{4,0},{1,5},{5,1},{2,6},{6,2},{3,7},{7,3},{8,12},{12,8},{9,1... | collective-permute-start | bytes 98312 | tf_op jit(solution)/shard_map/ppermute | solution.py:499
  79.6 2.5 %collective-permute-done.2 = f32[2,32,128]{2,1,0:T(8,128)S(1)} collective-permute-done((f32[2,32,128]{2,1,0:T(8,128)S(1)}, f32[2,32,128]{2,1,0:T(8,128)S(1)}, u32[]{:S(2)}, u32[]{:S(2)}) %collective-permute-start.2) | collective-permute-done | bytes 32800 | tf_op jit(solution)/shard_map/ppermute | solution.py:499
  82.1 0.0 copy-done.4
  82.1 0.6 bitcast_dynamic-update-slice_fusion
  (2 shorter events, 0.0 us)
Async XLA Ops:
  2.9 18.5 %copy-start.1 = (f32[4,32,128]{2,1,0:T(8,128)S(1)}, f32[4,32,128]{2,1,0:T(8,128)}, u32[]{:S(2)}) copy-start(f32[4,32,128]{2,1,0:T(8,128)} %get-tuple-element.17.refs_0_) | copy-start | bytes 196612
  2.9 8.8 %collective-permute-start = (f32[1,13,32,128]{3,2,1,0:T(8,128)}, f32[1,13,32,128]{3,2,1,0:T(8,128)S(1)}, u32[]{:S(2)}, u32[]{:S(2)}) collective-permute-start(f32[1,13,32,128]{3,2,1,0:T(8,128)} %bitcast.11), channel_id=1, source_target_pairs={{0,2},{2,0},{1,3},{3,1},{4,6},{6,4},{5,7},{7,5},{8,10},{10,8},{9,1... | collective-permute-start | bytes 638984 | tf_op jit(solution)/shard_map/ppermute | solution.py:431
  5.9 15.5 %all-to-all-start = ((f32[8,2,32,128]{3,2,1,0:T(8,128)}), f32[8,2,32,128]{3,2,1,0:T(8,128)S(1)}, u32[]{:S(2)}, u32[]{:S(2)}) async-start(f32[8,2,32,128]{3,2,1,0:T(8,128)} %bitcast.10), calls=%async_computation | async-start | bytes 524288 | tf_op jit(solution)/shard_map/all_to_all | solution.py:458
  12.7 1.8 %collective-permute-start.1 = (f32[2,13,32,128]{3,2,1,0:T(8,128)S(1)}, f32[2,13,32,128]{3,2,1,0:T(8,128)S(1)}, u32[]{:S(2)}, u32[]{:S(2)}) collective-permute-start(f32[2,13,32,128]{3,2,1,0:T(8,128)S(1)} %pad_maximum_fusion.refs_0_), channel_id=1, source_target_pairs={{0,1},{1,0},{2,3},{3,2},{4,5},{5,4},{6,7},{7,6},{8,9},{9,8},{10,11... | collective-permute-start | bytes 1277960 | tf_op jit(solution)/shard_map/ppermute | solution.py:431
  50.2 0.7 copy-start.2
  65.9 0.7 copy-start
  66.6 9.4 %all-to-all-start.4 = ((f32[8,2,32,128]{3,2,1,0:T(8,128)}), f32[8,2,32,128]{3,2,1,0:T(8,128)S(1)}, u32[]{:S(2)}, u32[]{:S(2)}) async-start(f32[8,2,32,128]{3,2,1,0:T(8,128)} %copy-done), calls=%async_computation.4 | async-start | bytes 524288 | tf_op jit(solution)/shard_map/all_to_all | solution.py:486
  76.0 1.0 %copy-start.3 = (f32[8,2,32,128]{3,2,1,0:T(8,128)S(1)}, f32[8,2,32,128]{3,2,1,0:T(8,128)}, u32[]{:S(2)}) copy-start(f32[8,2,32,128]{3,2,1,0:T(8,128)} %copy-done.2) | copy-start | bytes 786436
  78.1 4.0 %copy-start.4 = (f32[1,4,32,128]{3,2,1,0:T(8,128)}, f32[1,4,32,128]{3,2,1,0:T(8,128)S(1)}, u32[]{:S(2)}) copy-start(f32[1,4,32,128]{3,2,1,0:T(8,128)S(1)} %get-tuple-element.30) | copy-start | bytes 196612
  78.1 4.0 %collective-permute-start.2 = (f32[2,32,128]{2,1,0:T(8,128)S(1)}, f32[2,32,128]{2,1,0:T(8,128)S(1)}, u32[]{:S(2)}, u32[]{:S(2)}) collective-permute-start(f32[2,32,128]{2,1,0:T(8,128)S(1)} %get-tuple-element.29), channel_id=1, source_target_pairs={{0,4},{4,0},{1,5},{5,1},{2,6},{6,2},{3,7},{7,3},{8,12},{12,8},{9,1... | collective-permute-start | bytes 98312 | tf_op jit(solution)/shard_map/ppermute | solution.py:499
